TPU v7x, 32 devices: a whole 2x2x4 slice. The times are simulated.
32 devices in a mesh: section: 4 (over x, core), seq: 4 (over z), head: 2 (over y).
Axes of the slice: x: 2, y: 2, z: 4, core: 2. Of those that a mesh axis runs over, the one named last changes fastest.
Arguments:
- queries: bfloat16 [4, 512, 1536], P('section', 'seq', 'head'), may hold values from -240 to 240
- grad_out: bfloat16 [4, 512, 1536], P('section', 'seq', 'head'), may hold values from -96 to 96
- keys: bfloat16 [4, 256, 768], P('section', 'seq', 'head'), may hold values from -6 to 6
- values: bfloat16 [4, 256, 768], P('section', 'seq', 'head'), may hold values from -6 to 6
- proj_query: bfloat16 [4, 5376, 1536], P('section', None, 'head'), may hold values from -0.15625 to 0.15625
- section_span: int32 [4], replicated, may hold values from 0 to 3, each once
- span_prefix: int32 [4], replicated, may hold values from 128 to 256, as said below
Outputs:
- grad_input: bfloat16 [4, 5376, 512], P('section', 'head', 'seq')
- grad_key: bfloat16 [4, 256, 768], P('section', 'seq', 'head')
- grad_value: bfloat16 [4, 256, 768], P('section', 'seq', 'head')
Inputs may be any that keep to these rules, and one draw needn't show every extreme that they name: `span_prefix`: some entry equals 256 in every draw.
All inputs are finite; a program needn't handle non-finite values.
Results may differ from a plain program's by a relative error of at most 0.023.
Values may be sent and summed in bfloat16 or wider, within the bound.
No kernel may reach another device: no remote copies, remote signals or barrier semaphores. Data moves between devices by JAX's collectives and lax.ppermute only.
A program may use at most 64 MiB of HBM per device.

v0:
```python
import functools
import math

import jax
import jax.numpy as jnp
from jax import lax
from jax.experimental import pallas as pl
from jax.experimental.pallas import tpu as pltpu
from jax.sharding import PartitionSpec as P

HD = 128
MOST_PARTNERS = 4
STEPS_OF_FOUR = ((1, 3, 0, 2), (3, 2, 1, 0), (2, 0, 3, 1))
VMEM_LIMIT = 40 * 1024 * 1024

query_scale = 168.0 ** (-0.5)
exp2_scale = query_scale * math.log2(math.e)


def shifted(block, axis, distance):
    devices = range(lax.axis_size(axis))
    route = [((i - distance) % len(devices), i) for i in devices]
    return lax.ppermute(block, axis, route)


def seq_steps(n):
    if n == len(STEPS_OF_FOUR) + 1:
        return STEPS_OF_FOUR
    return [[(i + r) % n for i in range(n)] for r in range(1, n)]


def sent(block, step):
    return lax.ppermute(block, "seq", list(enumerate(step)))


def sent_back(block, step):
    return lax.ppermute(block, "seq", [(to, i) for i, to in enumerate(step)])


def dot(left, right, left_dim, right_dim):
    return lax.dot_general(
        left, right, (((left_dim,), (right_dim,)), ((), ())), preferred_element_type=jnp.float32
    )


def in_hbm(x):
    return pltpu.with_memory_space_constraint(x, pltpu.HBM)


def join_kernel(n_copies, key_ref, value_ref, grad_ref, *refs):
    *outs, grad_low, grad_high, sems = refs
    width, rows = key_ref.shape[2], grad_low.shape[0]
    pairs = [
        (key_ref.at[0], outs[0].at[:, :width]),
        (value_ref.at[0], outs[0].at[:, width:]),
        (grad_ref.at[0, :rows, :], grad_low),
        (grad_ref.at[0, rows:, :], grad_high),
    ]
    copies = [pltpu.make_async_copy(a, b, sems.at[i]) for i, (a, b) in enumerate(pairs)]
    for copy in copies:
        copy.start()
    for copy in copies[:2]:
        copy.wait()
    for out in outs[1:]:
        out[...] = outs[0][...]
    for copy in copies[2:]:
        copy.wait()


def stage_kernel(n_head, span_ref, prefix_ref, q_ref, w_ref, limit_out, q_out, *refs):
    *other_outs, span, prefix, sems, small_sems = refs
    feats = w_ref.shape[1] // n_head
    head = lax.axis_index("head")
    copies = []
    for r, out in enumerate(other_outs):
        start = pl.multiple_of(lax.rem(head + r + 1, n_head) * feats, 16)
        copies.append((w_ref.at[0, pl.ds(start, feats), :], out))
    copies.append((q_ref.at[0], q_out))
    copies = [pltpu.make_async_copy(a, b, sems.at[i]) for i, (a, b) in enumerate(copies)]
    small = [
        pltpu.make_async_copy(a, b, small_sems.at[i])
        for i, (a, b) in enumerate([(span_ref, span), (prefix_ref, prefix)])
    ]
    for copy in small + copies:
        copy.start()
    for copy in small:
        copy.wait()
    live = prefix[span[lax.axis_index("section")]]
    limit_out[...] = jnp.full(limit_out.shape, live, jnp.int32)
    for copy in copies:
        copy.wait()


def pair_of(refs, g):
    cols = [slice((2 * g + i) * HD, (2 * g + i + 1) * HD) for i in range(2)]
    return jnp.concatenate([ref[:, c] for c in cols for ref in refs], axis=0)


def cols_of(g, start=0):
    return slice(start + g * HD, start + (g + 1) * HD)


def attention_kernel(partners, n_other, limit_ref, q_ref, *refs):
    n_blocks = 1 + len(partners)
    kv_refs = refs[:n_blocks]
    d_low, d_high, *refs = refs[n_blocks:]
    w_refs = refs[:n_other]
    grad_ref, probs_ref, dscores_ref, *part_refs = refs[n_other:]

    held, both = kv_refs[0].shape
    width = both // 2
    seq = lax.axis_index("seq")
    owners = [seq if partners else 0]
    for step in partners:
        owners.append(sum(jnp.where(seq == to, i, 0) for i, to in enumerate(step)))
    spots = [i * held + lax.broadcasted_iota(jnp.int32, (held, 1), 0) for i in owners]
    alive = jnp.concatenate(spots, axis=0) < limit_ref[0:1, 0:1]

    rows = q_ref.shape[0]
    groups = range(width // HD)
    keys = [jnp.concatenate([ref[:, cols_of(g)] for ref in kv_refs], axis=0) for g in groups]
    scores = [dot(keys[g], pair_of((q_ref,), g), 1, 1) for g in groups]
    dprobs = []
    for g in groups:
        value = jnp.concatenate([ref[:, cols_of(g, width)] for ref in kv_refs], axis=0)
        dprobs.append(dot(value, pair_of((d_low, d_high), g), 1, 1))
    for g in groups:
        masked = jnp.where(alive, scores[g], jnp.float32(-1e30))
        top = jnp.max(masked, axis=0, keepdims=True)
        probs = jnp.exp2((masked - top) * exp2_scale)
        probs = probs * (1.0 / jnp.sum(probs, axis=0, keepdims=True))
        probs_low = probs.astype(jnp.bfloat16)
        delta = jnp.sum(probs_low.astype(jnp.float32) * dprobs[g], axis=0, keepdims=True)
        probs_ref[g] = probs_low
        dscores_ref[g] = (probs * (dprobs[g] - delta)).astype(jnp.bfloat16)
    for g in groups:
        grad_q = (query_scale * dot(keys[g], dscores_ref[g], 0, 0)).astype(jnp.bfloat16)
        for i in range(2):
            spot = (2 * g + i) * HD
            grad_ref[spot : spot + HD, :] = grad_q[:, i * rows : (i + 1) * rows]

    for w_ref, part_ref in zip(w_refs, part_refs):
        block = w_ref[: part_ref.shape[0], :]
        part_ref[...] = dot(block, grad_ref[...], 1, 0).astype(jnp.bfloat16)


def rest_kernel(n_other, grad_ref, *refs):
    for w_ref, part_ref in zip(refs[:n_other], refs[n_other:]):
        block = w_ref[w_ref.shape[0] - part_ref.shape[0] :, :]
        part_ref[...] = dot(block, grad_ref[...], 1, 0).astype(jnp.bfloat16)


def terms_kernel(probs_ref, dscores_ref, q_ref, d_low, d_high, *term_refs):
    held, both = term_refs[0].shape
    width = both // 2
    for g in range(width // HD):
        grad_k = (query_scale * dot(dscores_ref[g], pair_of((q_ref,), g), 1, 0)).astype(jnp.bfloat16)
        grad_v = dot(probs_ref[g], pair_of((d_low, d_high), g), 1, 0).astype(jnp.bfloat16)
        for r, ref in enumerate(term_refs):
            block = slice(r * held, (r + 1) * held)
            ref[:, g * HD : (g + 1) * HD] = grad_k[block]
            ref[:, width + g * HD : width + (g + 1) * HD] = grad_v[block]


def own_kernel(n_head, grad_ref, w_ref, out_ref, w_held, sem):
    feats = out_ref.shape[0]
    start = pl.multiple_of(lax.axis_index("head") * feats, 16)
    copy = pltpu.make_async_copy(w_ref.at[0, pl.ds(start, feats), :], w_held, sem)
    copy.start()
    copy.wait()
    out_ref[...] = dot(w_held[...], grad_ref[...], 1, 0)


def input_sum_kernel(n_other, start, own_ref, *refs):
    arrived = refs[:n_other]
    *_, out_ref, held, sem = refs
    at = slice(start, start + held.shape[0])
    total = own_ref[at, :]
    for ref in arrived:
        total = total + ref[...].astype(jnp.float32)
    held[...] = total.astype(jnp.bfloat16)
    copy = pltpu.make_async_copy(held, out_ref.at[0, at, :], sem)
    copy.start()
    copy.wait()


def term_sum_kernel(*refs):
    *terms, key_ref, value_ref = refs
    total = terms[0][...].astype(jnp.float32)
    for ref in terms[1:]:
        total = total + ref[...].astype(jnp.float32)
    low = total.astype(jnp.bfloat16)
    half = low.shape[1] // 2
    key_ref[0] = low[:, :half]
    value_ref[0] = low[:, half:]


VMEM = pl.BlockSpec(memory_space=pltpu.VMEM)
HBM = pl.BlockSpec(memory_space=pltpu.HBM)


def kernel_call(body, name, out_shape, in_specs, scratch=(), limit=VMEM_LIMIT):
    return pl.pallas_call(
        body,
        out_shape=out_shape,
        in_specs=in_specs,
        out_specs=jax.tree.map(lambda _: VMEM, out_shape),
        scratch_shapes=list(scratch),
        compiler_params=pltpu.CompilerParams(vmem_limit_bytes=limit),
        name=name,
    )


def on_device(queries, grad_out, keys, values, proj_query, section_span, span_prefix):
    n_seq, n_head = lax.axis_size("seq"), lax.axis_size("head")
    n_other = n_head - 1
    direct = n_seq <= MOST_PARTNERS
    low = jnp.bfloat16
    _, held, kv_width = keys.shape
    _, rows, width = queries.shape
    feats = proj_query.shape[1] // n_head

    def shape(*dims, dtype=low):
        return jax.ShapeDtypeStruct(dims, dtype)

    first = feats // 16 * 9 // 16 * 16
    partners = seq_steps(n_seq) if direct else []
    n_copies = 1 + len(partners)
    *joined, grad_low, grad_high = kernel_call(
        functools.partial(join_kernel, n_copies),
        "join",
        [shape(held, 2 * kv_width)] * n_copies + [shape(rows // 2, width)] * 2,
        [HBM] * 3,
        [pltpu.SemaphoreType.DMA((4,))],
    )(*[in_hbm(x) for x in (keys, values, grad_out)])
    if direct:
        blocks = joined[-1:] + [sent(x, step) for x, step in zip(joined, partners)]
    else:
        blocks = [lax.all_gather(joined[0], "seq", axis=0, tiled=True)]
    n_blocks, block_rows = len(blocks), blocks[0].shape[0]
    incoming = [shifted(part, "section", -1) for part in (grad_low, grad_high)]

    limit, q, *w_other = kernel_call(
        functools.partial(stage_kernel, n_head),
        "stage",
        [shape(8, HD, dtype=jnp.int32), shape(rows, width)] + [shape(feats, width)] * n_other,
        [HBM] * 4,
        [
            pltpu.SMEM(section_span.shape, jnp.int32),
            pltpu.SMEM(span_prefix.shape, jnp.int32),
            pltpu.SemaphoreType.DMA((1 + n_other,)),
            pltpu.SemaphoreType.DMA((2,)),
        ],
    )(*[in_hbm(x) for x in (section_span, span_prefix, queries, proj_query)])

    prefix = n_blocks * block_rows
    weights = shape(kv_width // HD, prefix, 2 * rows)
    grad_query, probs, dscores, *products = kernel_call(
        functools.partial(attention_kernel, partners, n_other),
        "attention",
        [shape(width, rows), weights, weights] + [shape(first, rows)] * n_other,
        [VMEM] * (4 + n_blocks + n_other),
    )(limit, q, *blocks, *incoming, *w_other)
    rest = kernel_call(
        functools.partial(rest_kernel, n_other),
        "rest",
        [shape(feats - first, rows)] * n_other,
        [VMEM] * (1 + n_other),
    )(grad_query, *w_other)
    arrived = [shifted(p, "head", r + 1) for part in (products, rest) for r, p in enumerate(part)]
    terms = kernel_call(
        terms_kernel, "terms", [shape(block_rows, 2 * kv_width)] * n_blocks, [VMEM] * 5
    )(probs, dscores, q, *incoming)
    if direct:
        all_terms = [terms[0]] + [sent_back(x, step) for x, step in zip(terms[1:], partners)]
    else:
        all_terms = [lax.psum_scatter(terms[0], "seq", scatter_dimension=0, tiled=True)]

    own = kernel_call(
        functools.partial(own_kernel, n_head),
        "own",
        shape(feats, rows, dtype=jnp.float32),
        [VMEM, HBM],
        [pltpu.VMEM((feats, width), low), pltpu.SemaphoreType.DMA(())],
    )(grad_query, in_hbm(proj_query))
    grad_key, grad_value = kernel_call(
        term_sum_kernel, "term_sum", [shape(1, held, kv_width)] * 2, [VMEM] * len(all_terms)
    )(*all_terms)
    grad_input = []
    for start, part in ((0, arrived[:n_other]), (first, arrived[n_other:])):
        grad_input = [
            pl.pallas_call(
                functools.partial(input_sum_kernel, n_other, start),
                out_shape=shape(1, feats, rows),
                in_specs=[VMEM] * (1 + n_other) + [HBM] * len(grad_input),
                out_specs=HBM,
                scratch_shapes=[pltpu.VMEM(part[0].shape, low), pltpu.SemaphoreType.DMA(())],
                input_output_aliases={1 + n_other: 0} if grad_input else {},
                compiler_params=pltpu.CompilerParams(vmem_limit_bytes=VMEM_LIMIT),
                name="input_sum",
            )(own, *part, *grad_input)
        ]
    grad_input = grad_input[0]
    return (grad_input, grad_key, grad_value)


def solution(mesh):
    in_specs = (
        P("section", "seq", "head"),
        P("section", "seq", "head"),
        P("section", "seq", "head"),
        P("section", "seq", "head"),
        P("section", None, "head"),
        P(),
        P(),
    )
    out_specs = (
        P("section", "head", "seq"),
        P("section", "seq", "head"),
        P("section", "seq", "head"),
    )
    return jax.shard_map(
        on_device, mesh=mesh, in_specs=in_specs, out_specs=out_specs, check_vma=False
    )
```

profile of v0, /device:TPU:0, one launch (start us, length us, event | category | flops | bytes accessed | tf_op | source)
XLA Modules:
  0.0 33.6 jit_solution(15162293634924279801)
XLA Ops:
  0.6 1.0 %join.1 = (bf16[64,768]{1,0:T(8,128)(2,1)S(1)}, bf16[64,768]{1,0:T(8,128)(2,1)S(1)}, bf16[64,768]{1,0:T(8,128)(2,1)S(1)}, bf16[64,768]{1,0:T(8,128)(2,1)S(1)}, b...) custom-call(bf16[1,64,384]{2,1,0:T(8,128)(2,1)} %key_ref.1, bf16[1,64,384]{2,1,0:T(8,128)(2,1)} %value_ref.1, ...), custom_call_target="tpu_custom_call" | custom-call | tf_op jit(solution)/shard_map/join/pallas_call | solution.py:229
  1.7 3.1 %collective-permute-start = (bf16[64,768]{1,0:T(8,128)(2,1)S(1)}, bf16[64,768]{1,0:T(8,128)(2,1)S(1)}, u32[]{:S(2)}, u32[]{:S(2)}) collective-permute-start(bf16[64,768]{1,0:T(8,128)(2,1)S(1)} %get-tuple-element.25), channel_id=1, source_target_pairs={{0,2},{2,6},{4,0},{6,4},{1,3},{3,7},{5,1},{7,5},{8,10},{10,14},{12... | collective-permute-start | bytes 294920 | tf_op jit(solution)/shard_map/ppermute | solution.py:33
  4.8 2.5 %collective-permute-start.1 = (bf16[64,768]{1,0:T(8,128)(2,1)S(1)}, bf16[64,768]{1,0:T(8,128)(2,1)S(1)}, u32[]{:S(2)}, u32[]{:S(2)}) collective-permute-start(bf16[64,768]{1,0:T(8,128)(2,1)S(1)} %get-tuple-element.26), channel_id=1, source_target_pairs={{0,6},{2,4},{4,2},{6,0},{1,7},{3,5},{5,3},{7,1},{8,14},{10,12},{12... | collective-permute-start | bytes 294920 | tf_op jit(solution)/shard_map/ppermute | solution.py:33
  7.2 1.6 %collective-permute-start.2 = (bf16[64,768]{1,0:T(8,128)(2,1)S(1)}, bf16[64,768]{1,0:T(8,128)(2,1)S(1)}, u32[]{:S(2)}, u32[]{:S(2)}) collective-permute-start(bf16[64,768]{1,0:T(8,128)(2,1)S(1)} %get-tuple-element.27), channel_id=1, source_target_pairs={{0,4},{2,0},{4,6},{6,2},{1,5},{3,1},{5,7},{7,3},{8,12},{10,8},{12,... | collective-permute-start | bytes 294920 | tf_op jit(solution)/shard_map/ppermute | solution.py:33
  8.8 0.1 collective-permute-start.3
  8.9 1.5 %collective-permute-start.4 = (bf16[64,768]{1,0:T(8,128)(2,1)S(1)}, bf16[64,768]{1,0:T(8,128)(2,1)S(1)}, u32[]{:S(2)}, u32[]{:S(2)}) collective-permute-start(bf16[64,768]{1,0:T(8,128)(2,1)S(1)} %get-tuple-element.29), channel_id=1, source_target_pairs={{8,0},{16,8},{24,16},{0,24},{9,1},{17,9},{25,17},{1,25},{10,2},{18... | collective-permute-start | bytes 294920 | tf_op jit(solution)/shard_map/ppermute | solution.py:23
  10.4 2.2 %stage.1 = (s32[8,128]{1,0:T(8,128)S(1)}, bf16[128,768]{1,0:T(8,128)(2,1)S(1)}, bf16[2688,768]{1,0:T(8,128)(2,1)S(1)}) custom-call(s32[4]{0:T(128)} %span_ref.1, s32[4]{0:T(128)} %prefix_ref.1, bf16[1,128,768]{2,1,0:T(8,128)(2,1)} %q_ref.1, bf16[1,5376,768]{2,1,0:T(8,128)(2,1)} %w_ref.3), custom_call_target="tpu_custom_call" | custom-call | tf_op jit(solution)/shard_map/stage/pallas_call | solution.py:243
  12.6 0.0 collective-permute-done.refs_1_
  12.6 0.4 %collective-permute-done.1.refs_2_ = bf16[64,768]{1,0:T(8,128)(2,1)S(1)} collective-permute-done((bf16[64,768]{1,0:T(8,128)(2,1)S(1)}, bf16[64,768]{1,0:T(8,128)(2,1)S(1)}, u32[]{:S(2)}, u32[]{:S(2)}) %collective-permute-start.1) | collective-permute-done | bytes 98336 | tf_op jit(solution)/shard_map/ppermute | solution.py:33
  13.1 0.0 collective-permute-done.2.refs_3_
  13.1 0.0 collective-permute-done.3.refs_4_.d_low
  13.1 0.0 collective-permute-done.4.refs_5_.d_high
  13.1 1.6 %attention.1 = (bf16[768,128]{1,0:T(8,128)(2,1)S(1)}, bf16[3,256,256]{2,1,0:T(8,128)(2,1)S(1)}, bf16[3,256,256]{2,1,0:T(8,128)(2,1)S(1)}, bf16[1504,128]{1,0:T(8,128)(2,1)S(1)}) custom-call(s32[8,128]{1,0:T(8,128)S(1)} %get-tuple-element.22.limit_ref, bf16[128,768]{1,0:T(8,128)(2,1)S(1)} %get-tuple-element.23.q_ref, ...), custom_call_target="tpu_custom_call" | custom-call | tf_op jit(solution)/shard_map/attention/pallas_call | solution.py:258
  14.7 1.6 %collective-permute-start.6 = (bf16[1504,128]{1,0:T(8,128)(2,1)S(1)}, bf16[1504,128]{1,0:T(8,128)(2,1)S(1)}, u32[]{:S(2)}, u32[]{:S(2)}) collective-permute-start(bf16[1504,128]{1,0:T(8,128)(2,1)S(1)} %get-tuple-element.32), channel_id=1, source_target_pairs={{1,0},{0,1},{3,2},{2,3},{5,4},{4,5},{7,6},{6,7},{9,8},{8,9},{11,10... | collective-permute-start | bytes 1155080 | tf_op jit(solution)/shard_map/ppermute | solution.py:23
  16.3 0.6 %rest.1 = bf16[1184,128]{1,0:T(8,128)(2,1)S(1)} custom-call(bf16[768,128]{1,0:T(8,128)(2,1)S(1)} %get-tuple-element.31.grad_ref, bf16[2688,768]{1,0:T(8,128)(2,1)S(1)} %get-tuple-element.30.refs_6_.refs_0_), custom_call_target="tpu_custom_call" | custom-call | tf_op jit(solution)/shard_map/rest/pallas_call | solution.py:264
  17.0 0.6 %collective-permute-start.5 = (bf16[1184,128]{1,0:T(8,128)(2,1)S(1)}, bf16[1184,128]{1,0:T(8,128)(2,1)S(1)}, u32[]{:S(2)}, u32[]{:S(2)}) collective-permute-start(bf16[1184,128]{1,0:T(8,128)(2,1)S(1)} %rest.1), channel_id=1, source_target_pairs={{1,0},{0,1},{3,2},{2,3},{5,4},{4,5},{7,6},{6,7},{9,8},{8,9},{11,10... | collective-permute-start | bytes 909320 | tf_op jit(solution)/shard_map/ppermute | solution.py:23
  17.6 0.4 %terms.1 = (bf16[64,768]{1,0:T(8,128)(2,1)S(1)}, bf16[64,768]{1,0:T(8,128)(2,1)S(1)}, bf16[64,768]{1,0:T(8,128)(2,1)S(1)}, bf16[64,768]{1,0:T(8,128)(2,1)S(1)}) custom-call(bf16[3,256,256]{2,1,0:T(8,128)(2,1)S(1)} %get-tuple-element.33.probs_ref, bf16[3,256,256]{2,1,0:T(8,128)(2,1)S(1)} %get-tuple-element.34.dscores_ref, ...), custom_call_target="tpu_custom_call" | custom-call | tf_op jit(solution)/shard_map/terms/pallas_call | solution.py:271
  17.9 4.6 %collective-permute-start.7 = (bf16[64,768]{1,0:T(8,128)(2,1)S(1)}, bf16[64,768]{1,0:T(8,128)(2,1)S(1)}, u32[]{:S(2)}, u32[]{:S(2)}) collective-permute-start(bf16[64,768]{1,0:T(8,128)(2,1)S(1)} %get-tuple-element.36), channel_id=1, source_target_pairs={{2,0},{6,2},{0,4},{4,6},{3,1},{7,3},{1,5},{5,7},{10,8},{14,10},{8,... | collective-permute-start | bytes 294920 | tf_op jit(solution)/shard_map/ppermute | solution.py:37
  22.5 0.4 %collective-permute-start.8 = (bf16[64,768]{1,0:T(8,128)(2,1)S(1)}, bf16[64,768]{1,0:T(8,128)(2,1)S(1)}, u32[]{:S(2)}, u32[]{:S(2)}) collective-permute-start(bf16[64,768]{1,0:T(8,128)(2,1)S(1)} %get-tuple-element.37), channel_id=1, source_target_pairs={{6,0},{4,2},{2,4},{0,6},{7,1},{5,3},{3,5},{1,7},{14,8},{12,10},{10... | collective-permute-start | bytes 294920 | tf_op jit(solution)/shard_map/ppermute | solution.py:37
  22.9 0.5 %collective-permute-start.9 = (bf16[64,768]{1,0:T(8,128)(2,1)S(1)}, bf16[64,768]{1,0:T(8,128)(2,1)S(1)}, u32[]{:S(2)}, u32[]{:S(2)}) collective-permute-start(bf16[64,768]{1,0:T(8,128)(2,1)S(1)} %get-tuple-element.38), channel_id=1, source_target_pairs={{4,0},{0,2},{6,4},{2,6},{5,1},{1,3},{7,5},{3,7},{12,8},{8,10},{14,... | collective-permute-start | bytes 294920 | tf_op jit(solution)/shard_map/ppermute | solution.py:37
  23.5 3.4 %own.1.own_ref = f32[2688,128]{1,0:T(8,128)S(1)} custom-call(bf16[768,128]{1,0:T(8,128)(2,1)S(1)} %get-tuple-element.31.grad_ref, bf16[1,5376,768]{2,1,0:T(8,128)(2,1)} %w_ref.3), custom_call_target="tpu_custom_call" | custom-call | tf_op jit(solution)/shard_map/own/pallas_call | solution.py:279
  26.9 0.0 collective-permute-done.7.refs_1_
  26.9 2.1 %collective-permute-done.8.refs_2_ = bf16[64,768]{1,0:T(8,128)(2,1)S(1)} collective-permute-done((bf16[64,768]{1,0:T(8,128)(2,1)S(1)}, bf16[64,768]{1,0:T(8,128)(2,1)S(1)}, u32[]{:S(2)}, u32[]{:S(2)}) %collective-permute-start.8) | collective-permute-done | bytes 98336 | tf_op jit(solution)/shard_map/ppermute | solution.py:37
  29.0 1.8 %collective-permute-done.9.refs_3_ = bf16[64,768]{1,0:T(8,128)(2,1)S(1)} collective-permute-done((bf16[64,768]{1,0:T(8,128)(2,1)S(1)}, bf16[64,768]{1,0:T(8,128)(2,1)S(1)}, u32[]{:S(2)}, u32[]{:S(2)}) %collective-permute-start.9) | collective-permute-done | bytes 98336 | tf_op jit(solution)/shard_map/ppermute | solution.py:37
  30.8 0.7 %term_sum.1 = (bf16[1,64,384]{2,1,0:T(8,128)(2,1)}, bf16[1,64,384]{2,1,0:T(8,128)(2,1)}) custom-call(bf16[64,768]{1,0:T(8,128)(2,1)S(1)} %get-tuple-element.35.refs_0_, bf16[64,768]{1,0:T(8,128)(2,1)S(1)} %collective-permute-done.7.refs_1_, bf16[64,768]{1,0:T(8,128)(2,1)S(1)} %collective-permute-done.8.refs_2_, ...), custom_call_target="tpu_custom_call" | custom-call | tf_op jit(solution)/shard_map/term_sum/pallas_call | solution.py:286
  31.5 0.0 collective-permute-done.6.refs_0_
  31.5 0.8 %input_sum.2.refs_1_ = bf16[1,2688,128]{2,1,0:T(8,128)(2,1)} custom-call(f32[2688,128]{1,0:T(8,128)S(1)} %own.1.own_ref, bf16[1504,128]{1,0:T(8,128)(2,1)S(1)} %collective-permute-done.6.refs_0_), custom_call_target="tpu_custom_call" | custom-call | tf_op jit(solution)/shard_map/input_sum/pallas_call | solution.py:292
  32.3 0.5 %collective-permute-done.5.refs_0_ = bf16[1184,128]{1,0:T(8,128)(2,1)S(1)} collective-permute-done((bf16[1184,128]{1,0:T(8,128)(2,1)S(1)}, bf16[1184,128]{1,0:T(8,128)(2,1)S(1)}, u32[]{:S(2)}, u32[]{:S(2)}) %collective-permute-start.5) | collective-permute-done | bytes 303136 | tf_op jit(solution)/shard_map/ppermute | solution.py:23
  32.8 0.8 %input_sum.3 = bf16[1,2688,128]{2,1,0:T(8,128)(2,1)} custom-call(f32[2688,128]{1,0:T(8,128)S(1)} %own.1.own_ref, bf16[1184,128]{1,0:T(8,128)(2,1)S(1)} %collective-permute-done.5.refs_0_, bf16[1,2688,128]{2,1,0:T(8,128)(2,1)} %input_sum.2.refs_1_), custom_call_target="tpu_custom_call", output_to_operand_aliasing={{}: (2, {})} | custom-call | tf_op jit(solution)/shard_map/input_sum/pallas_call | solution.py:292
Async XLA Ops:
  1.7 11.0 %collective-permute-start = (bf16[64,768]{1,0:T(8,128)(2,1)S(1)}, bf16[64,768]{1,0:T(8,128)(2,1)S(1)}, u32[]{:S(2)}, u32[]{:S(2)}) collective-permute-start(bf16[64,768]{1,0:T(8,128)(2,1)S(1)} %get-tuple-element.25), channel_id=1, source_target_pairs={{0,2},{2,6},{4,0},{6,4},{1,3},{3,7},{5,1},{7,5},{8,10},{10,14},{12... | collective-permute-start | bytes 294920 | tf_op jit(solution)/shard_map/ppermute | solution.py:33
  4.8 8.3 %collective-permute-start.1 = (bf16[64,768]{1,0:T(8,128)(2,1)S(1)}, bf16[64,768]{1,0:T(8,128)(2,1)S(1)}, u32[]{:S(2)}, u32[]{:S(2)}) collective-permute-start(bf16[64,768]{1,0:T(8,128)(2,1)S(1)} %get-tuple-element.26), channel_id=1, source_target_pairs={{0,6},{2,4},{4,2},{6,0},{1,7},{3,5},{5,3},{7,1},{8,14},{10,12},{12... | collective-permute-start | bytes 294920 | tf_op jit(solution)/shard_map/ppermute | solution.py:33
  7.2 5.9 %collective-permute-start.2 = (bf16[64,768]{1,0:T(8,128)(2,1)S(1)}, bf16[64,768]{1,0:T(8,128)(2,1)S(1)}, u32[]{:S(2)}, u32[]{:S(2)}) collective-permute-start(bf16[64,768]{1,0:T(8,128)(2,1)S(1)} %get-tuple-element.27), channel_id=1, source_target_pairs={{0,4},{2,0},{4,6},{6,2},{1,5},{3,1},{5,7},{7,3},{8,12},{10,8},{12,... | collective-permute-start | bytes 294920 | tf_op jit(solution)/shard_map/ppermute | solution.py:33
  8.8 4.3 %collective-permute-start.3 = (bf16[64,768]{1,0:T(8,128)(2,1)S(1)}, bf16[64,768]{1,0:T(8,128)(2,1)S(1)}, u32[]{:S(2)}, u32[]{:S(2)}) collective-permute-start(bf16[64,768]{1,0:T(8,128)(2,1)S(1)} %get-tuple-element.28), channel_id=1, source_target_pairs={{8,0},{16,8},{24,16},{0,24},{9,1},{17,9},{25,17},{1,25},{10,2},{18... | collective-permute-start | bytes 294920 | tf_op jit(solution)/shard_map/ppermute | solution.py:23
  8.9 4.2 %collective-permute-start.4 = (bf16[64,768]{1,0:T(8,128)(2,1)S(1)}, bf16[64,768]{1,0:T(8,128)(2,1)S(1)}, u32[]{:S(2)}, u32[]{:S(2)}) collective-permute-start(bf16[64,768]{1,0:T(8,128)(2,1)S(1)} %get-tuple-element.29), channel_id=1, source_target_pairs={{8,0},{16,8},{24,16},{0,24},{9,1},{17,9},{25,17},{1,25},{10,2},{18... | collective-permute-start | bytes 294920 | tf_op jit(solution)/shard_map/ppermute | solution.py:23
  14.7 16.7 %collective-permute-start.6 = (bf16[1504,128]{1,0:T(8,128)(2,1)S(1)}, bf16[1504,128]{1,0:T(8,128)(2,1)S(1)}, u32[]{:S(2)}, u32[]{:S(2)}) collective-permute-start(bf16[1504,128]{1,0:T(8,128)(2,1)S(1)} %get-tuple-element.32), channel_id=1, source_target_pairs={{1,0},{0,1},{3,2},{2,3},{5,4},{4,5},{7,6},{6,7},{9,8},{8,9},{11,10... | collective-permute-start | bytes 1155080 | tf_op jit(solution)/shard_map/ppermute | solution.py:23
  17.0 15.8 %collective-permute-start.5 = (bf16[1184,128]{1,0:T(8,128)(2,1)S(1)}, bf16[1184,128]{1,0:T(8,128)(2,1)S(1)}, u32[]{:S(2)}, u32[]{:S(2)}) collective-permute-start(bf16[1184,128]{1,0:T(8,128)(2,1)S(1)} %rest.1), channel_id=1, source_target_pairs={{1,0},{0,1},{3,2},{2,3},{5,4},{4,5},{7,6},{6,7},{9,8},{8,9},{11,10... | collective-permute-start | bytes 909320 | tf_op jit(solution)/shard_map/ppermute | solution.py:23
  17.9 9.0 %collective-permute-start.7 = (bf16[64,768]{1,0:T(8,128)(2,1)S(1)}, bf16[64,768]{1,0:T(8,128)(2,1)S(1)}, u32[]{:S(2)}, u32[]{:S(2)}) collective-permute-start(bf16[64,768]{1,0:T(8,128)(2,1)S(1)} %get-tuple-element.36), channel_id=1, source_target_pairs={{2,0},{6,2},{0,4},{4,6},{3,1},{7,3},{1,5},{5,7},{10,8},{14,10},{8,... | collective-permute-start | bytes 294920 | tf_op jit(solution)/shard_map/ppermute | solution.py:37
  22.5 6.5 %collective-permute-start.8 = (bf16[64,768]{1,0:T(8,128)(2,1)S(1)}, bf16[64,768]{1,0:T(8,128)(2,1)S(1)}, u32[]{:S(2)}, u32[]{:S(2)}) collective-permute-start(bf16[64,768]{1,0:T(8,128)(2,1)S(1)} %get-tuple-element.37), channel_id=1, source_target_pairs={{6,0},{4,2},{2,4},{0,6},{7,1},{5,3},{3,5},{1,7},{14,8},{12,10},{10... | collective-permute-start | bytes 294920 | tf_op jit(solution)/shard_map/ppermute | solution.py:37
  22.9 7.8 %collective-permute-start.9 = (bf16[64,768]{1,0:T(8,128)(2,1)S(1)}, bf16[64,768]{1,0:T(8,128)(2,1)S(1)}, u32[]{:S(2)}, u32[]{:S(2)}) collective-permute-start(bf16[64,768]{1,0:T(8,128)(2,1)S(1)} %get-tuple-element.38), channel_id=1, source_target_pairs={{4,0},{0,2},{6,4},{2,6},{5,1},{1,3},{7,5},{3,7},{12,8},{8,10},{14,... | collective-permute-start | bytes 294920 | tf_op jit(solution)/shard_map/ppermute | solution.py:37
where the time goes:
time: 33.8 us; the launch traced here: 33.6 us
  starting transfers between devices  16.5 us (49%)
  Pallas kernels  11.6 us (34%)
  waiting for transfers between devices  4.81 us (14%)
  between operations  0.71 us (2%)
    ppermute x3, starting transfers between devices, sent(): return lax.ppermute(block, 'seq', list(enumerate(step)))  7.13 us
    ppermute x3, starting transfers between devices, sent_back(): return lax.ppermute(block, 'seq', [(to, i) for i, to in enumerate(step)])  5.57 us
    ppermute x3, waiting for transfers between devices, sent_back(): return lax.ppermute(block, 'seq', [(to, i) for i, to in enumerate(step)])  3.86 us
    ppermute x4, starting transfers between devices, shifted(): return lax.ppermute(block, axis, route)  3.79 us
    pallas_call x1, Pallas kernels, on_device(): kernel_call(functools.partial(own_kernel, n_head), 'own', shape(feats, ro...  3.42 us
    pallas_call x1, Pallas kernels, on_device(): kernel_call(functools.partial(stage_kernel, n_head), 'stage', [shape(8, H...  2.21 us
    pallas_call x1, Pallas kernels, on_device(): kernel_call(functools.partial(attention_kernel, partners, n_other), 'atte...  1.63 us
    pallas_call x2, Pallas kernels, on_device(): pl.pallas_call(functools.partial(input_sum_kernel, n_other, start), out_s...  1.61 us
  transfers between devices with their start and end apart: 10, of which 4 were waited for; matrix products, arithmetic and copies ran while one was open for 0% of the time, Pallas kernels for 24%

commit v1 on v0

--- a/solution.py
+++ b/solution.py
@@ -101,9 +101,10 @@
 
 
 def attention_kernel(partners, n_other, limit_ref, q_ref, *refs):
-    n_blocks = 1 + len(partners)
-    kv_refs = refs[:n_blocks]
-    d_low, d_high, *refs = refs[n_blocks:]
+    most = 1 + len(partners[:-1])
+    kv_refs, (d_low, d_high), refs = refs[:most], refs[most : most + 2], refs[most + 2 :]
+    if partners:
+        kv_refs, refs = kv_refs + refs[:1], refs[1:]
     w_refs = refs[:n_other]
     grad_ref, probs_ref, dscores_ref, *part_refs = refs[n_other:]
 
@@ -234,11 +235,12 @@
         [pltpu.SemaphoreType.DMA((4,))],
     )(*[in_hbm(x) for x in (keys, values, grad_out)])
     if direct:
-        blocks = joined[-1:] + [sent(x, step) for x, step in zip(joined, partners)]
+        blocks = joined[-1:] + [sent(x, step) for x, step in zip(joined, partners[:-1])]
     else:
         blocks = [lax.all_gather(joined[0], "seq", axis=0, tiled=True)]
-    n_blocks, block_rows = len(blocks), blocks[0].shape[0]
     incoming = [shifted(part, "section", -1) for part in (grad_low, grad_high)]
+    last = [sent(joined[len(partners) - 1], step) for step in partners[-1:]]
+    n_blocks, block_rows = len(blocks) + len(last), blocks[0].shape[0]
 
     limit, q, *w_other = kernel_call(
         functools.partial(stage_kernel, n_head),
@@ -260,7 +262,7 @@
         "attention",
         [shape(width, rows), weights, weights] + [shape(first, rows)] * n_other,
         [VMEM] * (4 + n_blocks + n_other),
-    )(limit, q, *blocks, *incoming, *w_other)
+    )(limit, q, *blocks, *incoming, *last, *w_other)
     rest = kernel_call(
         functools.partial(rest_kernel, n_other),
         "rest",

time: 33.8 us -> 33.3 us (0.985)
  starting transfers between devices: 16.5 us -> 15.7 us
    ppermute x3, waiting for transfers between devices: 0.45 us -> 1.22 us  [sent(): return lax.ppermute(block, 'seq', list(enumerate(step)))]
    ppermute x3, starting transfers between devices: 5.57 us -> 4.8 us  [sent_back(): return lax.ppermute(block, 'seq', [(to, i) for i, to in enumerate(step)])]
    ppermute x4, waiting for transfers between devices: 0.5 us -> 0.05 us  [shifted(): return lax.ppermute(block, axis, route)]
  transfers between devices with their start and end apart: 10 -> 10, of which waited for: 4 -> 3; matrix products, arithmetic and copies ran while one was open for 0% -> 0% of each run, Pallas kernels for 24% -> 25%
where the time goes in v1:
time: 33.3 us; the launch traced here: 33.1 us
  starting transfers between devices  15.7 us (47%)
  Pallas kernels  11.6 us (35%)
  waiting for transfers between devices  5.14 us (15%)
  between operations  0.73 us (2%)
    ppermute x3, starting transfers between devices, sent(): return lax.ppermute(block, 'seq', list(enumerate(step)))  7.13 us
    ppermute x3, starting transfers between devices, sent_back(): return lax.ppermute(block, 'seq', [(to, i) for i, to in enumerate(step)])  4.8 us
    ppermute x3, waiting for transfers between devices, sent_back(): return lax.ppermute(block, 'seq', [(to, i) for i, to in enumerate(step)])  3.86 us
    ppermute x4, starting transfers between devices, shifted(): return lax.ppermute(block, axis, route)  3.76 us
    pallas_call x1, Pallas kernels, on_device(): kernel_call(functools.partial(own_kernel, n_head), 'own', shape(feats, ro...  3.42 us
    pallas_call x1, Pallas kernels, on_device(): kernel_call(functools.partial(stage_kernel, n_head), 'stage', [shape(8, H...  2.21 us
    pallas_call x1, Pallas kernels, on_device(): kernel_call(functools.partial(attention_kernel, partners, n_other), 'atte...  1.63 us
    pallas_call x2, Pallas kernels, on_device(): pl.pallas_call(functools.partial(input_sum_kernel, n_other, start), out_s...  1.61 us
  transfers between devices with their start and end apart: 10, of which 3 were waited for; matrix products, arithmetic and copies ran while one was open for 0% of the time, Pallas kernels for 25%

profile of v1, /device:TPU:0, one launch (start us, length us, event | category | flops | bytes accessed | tf_op | source)
XLA Modules:
  0.0 33.1 jit_solution(9923332674440667457)
XLA Ops:
  0.6 1.0 %join.1 = (bf16[64,768]{1,0:T(8,128)(2,1)S(1)}, bf16[64,768]{1,0:T(8,128)(2,1)S(1)}, bf16[64,768]{1,0:T(8,128)(2,1)S(1)}, bf16[64,768]{1,0:T(8,128)(2,1)S(1)}, b...) custom-call(bf16[1,64,384]{2,1,0:T(8,128)(2,1)} %key_ref.1, bf16[1,64,384]{2,1,0:T(8,128)(2,1)} %value_ref.1, ...), custom_call_target="tpu_custom_call" | custom-call | tf_op jit(solution)/shard_map/join/pallas_call | solution.py:230
  1.7 3.1 %collective-permute-start = (bf16[64,768]{1,0:T(8,128)(2,1)S(1)}, bf16[64,768]{1,0:T(8,128)(2,1)S(1)}, u32[]{:S(2)}, u32[]{:S(2)}) collective-permute-start(bf16[64,768]{1,0:T(8,128)(2,1)S(1)} %get-tuple-element.25), channel_id=1, source_target_pairs={{0,2},{2,6},{4,0},{6,4},{1,3},{3,7},{5,1},{7,5},{8,10},{10,14},{12... | collective-permute-start | bytes 294920 | tf_op jit(solution)/shard_map/ppermute | solution.py:33
  4.8 2.5 %collective-permute-start.1 = (bf16[64,768]{1,0:T(8,128)(2,1)S(1)}, bf16[64,768]{1,0:T(8,128)(2,1)S(1)}, u32[]{:S(2)}, u32[]{:S(2)}) collective-permute-start(bf16[64,768]{1,0:T(8,128)(2,1)S(1)} %get-tuple-element.26), channel_id=1, source_target_pairs={{0,6},{2,4},{4,2},{6,0},{1,7},{3,5},{5,3},{7,1},{8,14},{10,12},{12... | collective-permute-start | bytes 294920 | tf_op jit(solution)/shard_map/ppermute | solution.py:33
  7.2 0.4 %collective-permute-start.2 = (bf16[64,768]{1,0:T(8,128)(2,1)S(1)}, bf16[64,768]{1,0:T(8,128)(2,1)S(1)}, u32[]{:S(2)}, u32[]{:S(2)}) collective-permute-start(bf16[64,768]{1,0:T(8,128)(2,1)S(1)} %get-tuple-element.27), channel_id=1, source_target_pairs={{8,0},{16,8},{24,16},{0,24},{9,1},{17,9},{25,17},{1,25},{10,2},{18... | collective-permute-start | bytes 294920 | tf_op jit(solution)/shard_map/ppermute | solution.py:23
  7.6 1.2 %collective-permute-start.3 = (bf16[64,768]{1,0:T(8,128)(2,1)S(1)}, bf16[64,768]{1,0:T(8,128)(2,1)S(1)}, u32[]{:S(2)}, u32[]{:S(2)}) collective-permute-start(bf16[64,768]{1,0:T(8,128)(2,1)S(1)} %get-tuple-element.28), channel_id=1, source_target_pairs={{8,0},{16,8},{24,16},{0,24},{9,1},{17,9},{25,17},{1,25},{10,2},{18... | collective-permute-start | bytes 294920 | tf_op jit(solution)/shard_map/ppermute | solution.py:23
  8.8 1.6 %collective-permute-start.4 = (bf16[64,768]{1,0:T(8,128)(2,1)S(1)}, bf16[64,768]{1,0:T(8,128)(2,1)S(1)}, u32[]{:S(2)}, u32[]{:S(2)}) collective-permute-start(bf16[64,768]{1,0:T(8,128)(2,1)S(1)} %get-tuple-element.29), channel_id=1, source_target_pairs={{0,4},{2,0},{4,6},{6,2},{1,5},{3,1},{5,7},{7,3},{8,12},{10,8},{12,... | collective-permute-start | bytes 294920 | tf_op jit(solution)/shard_map/ppermute | solution.py:33
  10.4 2.2 %stage.1 = (s32[8,128]{1,0:T(8,128)S(1)}, bf16[128,768]{1,0:T(8,128)(2,1)S(1)}, bf16[2688,768]{1,0:T(8,128)(2,1)S(1)}) custom-call(s32[4]{0:T(128)} %span_ref.1, s32[4]{0:T(128)} %prefix_ref.1, bf16[1,128,768]{2,1,0:T(8,128)(2,1)} %q_ref.1, bf16[1,5376,768]{2,1,0:T(8,128)(2,1)} %w_ref.3), custom_call_target="tpu_custom_call" | custom-call | tf_op jit(solution)/shard_map/stage/pallas_call | solution.py:245
  12.6 0.0 collective-permute-done.refs_1_
  12.6 0.0 collective-permute-done.1.refs_2_
  12.6 0.0 collective-permute-done.2.refs_3_.d_low
  12.7 0.0 collective-permute-done.3.refs_4_.d_high
  12.7 1.2 %collective-permute-done.4.refs_5_ = bf16[64,768]{1,0:T(8,128)(2,1)S(1)} collective-permute-done((bf16[64,768]{1,0:T(8,128)(2,1)S(1)}, bf16[64,768]{1,0:T(8,128)(2,1)S(1)}, u32[]{:S(2)}, u32[]{:S(2)}) %collective-permute-start.4) | collective-permute-done | bytes 98336 | tf_op jit(solution)/shard_map/ppermute | solution.py:33
  13.9 1.6 %attention.1 = (bf16[768,128]{1,0:T(8,128)(2,1)S(1)}, bf16[3,256,256]{2,1,0:T(8,128)(2,1)S(1)}, bf16[3,256,256]{2,1,0:T(8,128)(2,1)S(1)}, bf16[1504,128]{1,0:T(8,128)(2,1)S(1)}) custom-call(s32[8,128]{1,0:T(8,128)S(1)} %get-tuple-element.22.limit_ref, bf16[128,768]{1,0:T(8,128)(2,1)S(1)} %get-tuple-element.23.q_ref, ...), custom_call_target="tpu_custom_call" | custom-call | tf_op jit(solution)/shard_map/attention/pallas_call | solution.py:260
  15.5 1.6 %collective-permute-start.6 = (bf16[1504,128]{1,0:T(8,128)(2,1)S(1)}, bf16[1504,128]{1,0:T(8,128)(2,1)S(1)}, u32[]{:S(2)}, u32[]{:S(2)}) collective-permute-start(bf16[1504,128]{1,0:T(8,128)(2,1)S(1)} %get-tuple-element.32), channel_id=1, source_target_pairs={{1,0},{0,1},{3,2},{2,3},{5,4},{4,5},{7,6},{6,7},{9,8},{8,9},{11,10... | collective-permute-start | bytes 1155080 | tf_op jit(solution)/shard_map/ppermute | solution.py:23
  17.1 0.6 %rest.1 = bf16[1184,128]{1,0:T(8,128)(2,1)S(1)} custom-call(bf16[768,128]{1,0:T(8,128)(2,1)S(1)} %get-tuple-element.31.grad_ref, bf16[2688,768]{1,0:T(8,128)(2,1)S(1)} %get-tuple-element.30.refs_6_.refs_0_), custom_call_target="tpu_custom_call" | custom-call | tf_op jit(solution)/shard_map/rest/pallas_call | solution.py:266
  17.8 0.6 %collective-permute-start.5 = (bf16[1184,128]{1,0:T(8,128)(2,1)S(1)}, bf16[1184,128]{1,0:T(8,128)(2,1)S(1)}, u32[]{:S(2)}, u32[]{:S(2)}) collective-permute-start(bf16[1184,128]{1,0:T(8,128)(2,1)S(1)} %rest.1), channel_id=1, source_target_pairs={{1,0},{0,1},{3,2},{2,3},{5,4},{4,5},{7,6},{6,7},{9,8},{8,9},{11,10... | collective-permute-start | bytes 909320 | tf_op jit(solution)/shard_map/ppermute | solution.py:23
  18.3 0.4 %terms.1 = (bf16[64,768]{1,0:T(8,128)(2,1)S(1)}, bf16[64,768]{1,0:T(8,128)(2,1)S(1)}, bf16[64,768]{1,0:T(8,128)(2,1)S(1)}, bf16[64,768]{1,0:T(8,128)(2,1)S(1)}) custom-call(bf16[3,256,256]{2,1,0:T(8,128)(2,1)S(1)} %get-tuple-element.33.probs_ref, bf16[3,256,256]{2,1,0:T(8,128)(2,1)S(1)} %get-tuple-element.34.dscores_ref, ...), custom_call_target="tpu_custom_call" | custom-call | tf_op jit(solution)/shard_map/terms/pallas_call | solution.py:273
  18.7 3.8 %collective-permute-start.7 = (bf16[64,768]{1,0:T(8,128)(2,1)S(1)}, bf16[64,768]{1,0:T(8,128)(2,1)S(1)}, u32[]{:S(2)}, u32[]{:S(2)}) collective-permute-start(bf16[64,768]{1,0:T(8,128)(2,1)S(1)} %get-tuple-element.36), channel_id=1, source_target_pairs={{2,0},{6,2},{0,4},{4,6},{3,1},{7,3},{1,5},{5,7},{10,8},{14,10},{8,... | collective-permute-start | bytes 294920 | tf_op jit(solution)/shard_map/ppermute | solution.py:37
  22.5 0.4 %collective-permute-start.8 = (bf16[64,768]{1,0:T(8,128)(2,1)S(1)}, bf16[64,768]{1,0:T(8,128)(2,1)S(1)}, u32[]{:S(2)}, u32[]{:S(2)}) collective-permute-start(bf16[64,768]{1,0:T(8,128)(2,1)S(1)} %get-tuple-element.37), channel_id=1, source_target_pairs={{6,0},{4,2},{2,4},{0,6},{7,1},{5,3},{3,5},{1,7},{14,8},{12,10},{10... | collective-permute-start | bytes 294920 | tf_op jit(solution)/shard_map/ppermute | solution.py:37
  22.9 0.5 %collective-permute-start.9 = (bf16[64,768]{1,0:T(8,128)(2,1)S(1)}, bf16[64,768]{1,0:T(8,128)(2,1)S(1)}, u32[]{:S(2)}, u32[]{:S(2)}) collective-permute-start(bf16[64,768]{1,0:T(8,128)(2,1)S(1)} %get-tuple-element.38), channel_id=1, source_target_pairs={{4,0},{0,2},{6,4},{2,6},{5,1},{1,3},{7,5},{3,7},{12,8},{8,10},{14,... | collective-permute-start | bytes 294920 | tf_op jit(solution)/shard_map/ppermute | solution.py:37
  23.5 3.4 %own.1.own_ref = f32[2688,128]{1,0:T(8,128)S(1)} custom-call(bf16[768,128]{1,0:T(8,128)(2,1)S(1)} %get-tuple-element.31.grad_ref, bf16[1,5376,768]{2,1,0:T(8,128)(2,1)} %w_ref.3), custom_call_target="tpu_custom_call" | custom-call | tf_op jit(solution)/shard_map/own/pallas_call | solution.py:281
  26.9 0.0 collective-permute-done.7.refs_1_
  26.9 2.1 %collective-permute-done.8.refs_2_ = bf16[64,768]{1,0:T(8,128)(2,1)S(1)} collective-permute-done((bf16[64,768]{1,0:T(8,128)(2,1)S(1)}, bf16[64,768]{1,0:T(8,128)(2,1)S(1)}, u32[]{:S(2)}, u32[]{:S(2)}) %collective-permute-start.8) | collective-permute-done | bytes 98336 | tf_op jit(solution)/shard_map/ppermute | solution.py:37
  29.0 1.8 %collective-permute-done.9.refs_3_ = bf16[64,768]{1,0:T(8,128)(2,1)S(1)} collective-permute-done((bf16[64,768]{1,0:T(8,128)(2,1)S(1)}, bf16[64,768]{1,0:T(8,128)(2,1)S(1)}, u32[]{:S(2)}, u32[]{:S(2)}) %collective-permute-start.9) | collective-permute-done | bytes 98336 | tf_op jit(solution)/shard_map/ppermute | solution.py:37
  30.8 0.7 %term_sum.1 = (bf16[1,64,384]{2,1,0:T(8,128)(2,1)}, bf16[1,64,384]{2,1,0:T(8,128)(2,1)}) custom-call(bf16[64,768]{1,0:T(8,128)(2,1)S(1)} %get-tuple-element.35.refs_0_, bf16[64,768]{1,0:T(8,128)(2,1)S(1)} %collective-permute-done.7.refs_1_, bf16[64,768]{1,0:T(8,128)(2,1)S(1)} %collective-permute-done.8.refs_2_, ...), custom_call_target="tpu_custom_call" | custom-call | tf_op jit(solution)/shard_map/term_sum/pallas_call | solution.py:288
  31.5 0.0 collective-permute-done.6.refs_0_
  31.5 0.8 %input_sum.2.refs_1_ = bf16[1,2688,128]{2,1,0:T(8,128)(2,1)} custom-call(f32[2688,128]{1,0:T(8,128)S(1)} %own.1.own_ref, bf16[1504,128]{1,0:T(8,128)(2,1)S(1)} %collective-permute-done.6.refs_0_), custom_call_target="tpu_custom_call" | custom-call | tf_op jit(solution)/shard_map/input_sum/pallas_call | solution.py:294
  32.3 0.0 collective-permute-done.5.refs_0_
  32.3 0.8 %input_sum.3 = bf16[1,2688,128]{2,1,0:T(8,128)(2,1)} custom-call(f32[2688,128]{1,0:T(8,128)S(1)} %own.1.own_ref, bf16[1184,128]{1,0:T(8,128)(2,1)S(1)} %collective-permute-done.5.refs_0_, bf16[1,2688,128]{2,1,0:T(8,128)(2,1)} %input_sum.2.refs_1_), custom_call_target="tpu_custom_call", output_to_operand_aliasing={{}: (2, {})} | custom-call | tf_op jit(solution)/shard_map/input_sum/pallas_call | solution.py:294
Async XLA Ops:
  1.7 11.0 %collective-permute-start = (bf16[64,768]{1,0:T(8,128)(2,1)S(1)}, bf16[64,768]{1,0:T(8,128)(2,1)S(1)}, u32[]{:S(2)}, u32[]{:S(2)}) collective-permute-start(bf16[64,768]{1,0:T(8,128)(2,1)S(1)} %get-tuple-element.25), channel_id=1, source_target_pairs={{0,2},{2,6},{4,0},{6,4},{1,3},{3,7},{5,1},{7,5},{8,10},{10,14},{12... | collective-permute-start | bytes 294920 | tf_op jit(solution)/shard_map/ppermute | solution.py:33
  4.8 7.9 %collective-permute-start.1 = (bf16[64,768]{1,0:T(8,128)(2,1)S(1)}, bf16[64,768]{1,0:T(8,128)(2,1)S(1)}, u32[]{:S(2)}, u32[]{:S(2)}) collective-permute-start(bf16[64,768]{1,0:T(8,128)(2,1)S(1)} %get-tuple-element.26), channel_id=1, source_target_pairs={{0,6},{2,4},{4,2},{6,0},{1,7},{3,5},{5,3},{7,1},{8,14},{10,12},{12... | collective-permute-start | bytes 294920 | tf_op jit(solution)/shard_map/ppermute | solution.py:33
  7.2 5.4 %collective-permute-start.2 = (bf16[64,768]{1,0:T(8,128)(2,1)S(1)}, bf16[64,768]{1,0:T(8,128)(2,1)S(1)}, u32[]{:S(2)}, u32[]{:S(2)}) collective-permute-start(bf16[64,768]{1,0:T(8,128)(2,1)S(1)} %get-tuple-element.27), channel_id=1, source_target_pairs={{8,0},{16,8},{24,16},{0,24},{9,1},{17,9},{25,17},{1,25},{10,2},{18... | collective-permute-start | bytes 294920 | tf_op jit(solution)/shard_map/ppermute | solution.py:23
  7.6 5.1 %collective-permute-start.3 = (bf16[64,768]{1,0:T(8,128)(2,1)S(1)}, bf16[64,768]{1,0:T(8,128)(2,1)S(1)}, u32[]{:S(2)}, u32[]{:S(2)}) collective-permute-start(bf16[64,768]{1,0:T(8,128)(2,1)S(1)} %get-tuple-element.28), channel_id=1, source_target_pairs={{8,0},{16,8},{24,16},{0,24},{9,1},{17,9},{25,17},{1,25},{10,2},{18... | collective-permute-start | bytes 294920 | tf_op jit(solution)/shard_map/ppermute | solution.py:23
  8.8 5.0 %collective-permute-start.4 = (bf16[64,768]{1,0:T(8,128)(2,1)S(1)}, bf16[64,768]{1,0:T(8,128)(2,1)S(1)}, u32[]{:S(2)}, u32[]{:S(2)}) collective-permute-start(bf16[64,768]{1,0:T(8,128)(2,1)S(1)} %get-tuple-element.29), channel_id=1, source_target_pairs={{0,4},{2,0},{4,6},{6,2},{1,5},{3,1},{5,7},{7,3},{8,12},{10,8},{12,... | collective-permute-start | bytes 294920 | tf_op jit(solution)/shard_map/ppermute | solution.py:33
  15.5 15.9 %collective-permute-start.6 = (bf16[1504,128]{1,0:T(8,128)(2,1)S(1)}, bf16[1504,128]{1,0:T(8,128)(2,1)S(1)}, u32[]{:S(2)}, u32[]{:S(2)}) collective-permute-start(bf16[1504,128]{1,0:T(8,128)(2,1)S(1)} %get-tuple-element.32), channel_id=1, source_target_pairs={{1,0},{0,1},{3,2},{2,3},{5,4},{4,5},{7,6},{6,7},{9,8},{8,9},{11,10... | collective-permute-start | bytes 1155080 | tf_op jit(solution)/shard_map/ppermute | solution.py:23
  17.8 14.6 %collective-permute-start.5 = (bf16[1184,128]{1,0:T(8,128)(2,1)S(1)}, bf16[1184,128]{1,0:T(8,128)(2,1)S(1)}, u32[]{:S(2)}, u32[]{:S(2)}) collective-permute-start(bf16[1184,128]{1,0:T(8,128)(2,1)S(1)} %rest.1), channel_id=1, source_target_pairs={{1,0},{0,1},{3,2},{2,3},{5,4},{4,5},{7,6},{6,7},{9,8},{8,9},{11,10... | collective-permute-start | bytes 909320 | tf_op jit(solution)/shard_map/ppermute | solution.py:23
  18.7 8.2 %collective-permute-start.7 = (bf16[64,768]{1,0:T(8,128)(2,1)S(1)}, bf16[64,768]{1,0:T(8,128)(2,1)S(1)}, u32[]{:S(2)}, u32[]{:S(2)}) collective-permute-start(bf16[64,768]{1,0:T(8,128)(2,1)S(1)} %get-tuple-element.36), channel_id=1, source_target_pairs={{2,0},{6,2},{0,4},{4,6},{3,1},{7,3},{1,5},{5,7},{10,8},{14,10},{8,... | collective-permute-start | bytes 294920 | tf_op jit(solution)/shard_map/ppermute | solution.py:37
  22.5 6.5 %collective-permute-start.8 = (bf16[64,768]{1,0:T(8,128)(2,1)S(1)}, bf16[64,768]{1,0:T(8,128)(2,1)S(1)}, u32[]{:S(2)}, u32[]{:S(2)}) collective-permute-start(bf16[64,768]{1,0:T(8,128)(2,1)S(1)} %get-tuple-element.37), channel_id=1, source_target_pairs={{6,0},{4,2},{2,4},{0,6},{7,1},{5,3},{3,5},{1,7},{14,8},{12,10},{10... | collective-permute-start | bytes 294920 | tf_op jit(solution)/shard_map/ppermute | solution.py:37
  22.9 7.8 %collective-permute-start.9 = (bf16[64,768]{1,0:T(8,128)(2,1)S(1)}, bf16[64,768]{1,0:T(8,128)(2,1)S(1)}, u32[]{:S(2)}, u32[]{:S(2)}) collective-permute-start(bf16[64,768]{1,0:T(8,128)(2,1)S(1)} %get-tuple-element.38), channel_id=1, source_target_pairs={{4,0},{0,2},{6,4},{2,6},{5,1},{1,3},{7,5},{3,7},{12,8},{8,10},{14,... | collective-permute-start | bytes 294920 | tf_op jit(solution)/shard_map/ppermute | solution.py:37

commit v2 on v1

--- a/solution.py
+++ b/solution.py
@@ -10,7 +10,7 @@
 
 HD = 128
 MOST_PARTNERS = 4
-STEPS_OF_FOUR = ((1, 3, 0, 2), (3, 2, 1, 0), (2, 0, 3, 1))
+STEPS_OF_FOUR = ((1, 3, 0, 2), (2, 0, 3, 1), (3, 2, 1, 0))
 VMEM_LIMIT = 40 * 1024 * 1024
 
 query_scale = 168.0 ** (-0.5)

time: 33.3 us -> 33.7 us (1.012)
  starting transfers between devices: 15.7 us -> 17.2 us
  waiting for transfers between devices: 5.14 us -> 3.93 us
    ppermute x3, waiting for transfers between devices: 3.86 us -> 2.81 us  [sent_back(): return lax.ppermute(block, 'seq', [(to, i) for i, to in enumerate(step)])]
    ppermute x3, starting transfers between devices: 4.8 us -> 5.46 us  [sent_back(): return lax.ppermute(block, 'seq', [(to, i) for i, to in enumerate(step)])]
    ppermute x3, starting transfers between devices: 7.13 us -> 7.76 us  [sent(): return lax.ppermute(block, 'seq', list(enumerate(step)))]
  transfers between devices with their start and end apart: 10 -> 10, of which waited for: 3 -> 3; matrix products, arithmetic and copies ran while one was open for 0% -> 0% of each run, Pallas kernels for 25% -> 24%
where the time goes in v2:
time: 33.7 us; the launch traced here: 33.5 us
  starting transfers between devices  17.2 us (51%)
  Pallas kernels  11.6 us (34%)
  waiting for transfers between devices  3.93 us (12%)
  between operations  0.73 us (2%)
    ppermute x3, starting transfers between devices, sent(): return lax.ppermute(block, 'seq', list(enumerate(step)))  7.76 us
    ppermute x3, starting transfers between devices, sent_back(): return lax.ppermute(block, 'seq', [(to, i) for i, to in enumerate(step)])  5.46 us
    ppermute x4, starting transfers between devices, shifted(): return lax.ppermute(block, axis, route)  4.04 us
    pallas_call x1, Pallas kernels, on_device(): kernel_call(functools.partial(own_kernel, n_head), 'own', shape(feats, ro...  3.41 us
    ppermute x3, waiting for transfers between devices, sent_back(): return lax.ppermute(block, 'seq', [(to, i) for i, to in enumerate(step)])  2.81 us
    pallas_call x1, Pallas kernels, on_device(): kernel_call(functools.partial(stage_kernel, n_head), 'stage', [shape(8, H...  2.21 us
    pallas_call x1, Pallas kernels, on_device(): kernel_call(functools.partial(attention_kernel, partners, n_other), 'atte...  1.62 us
    pallas_call x2, Pallas kernels, on_device(): pl.pallas_call(functools.partial(input_sum_kernel, n_other, start), out_s...  1.61 us
  transfers between devices with their start and end apart: 10, of which 3 were waited for; matrix products, arithmetic and copies ran while one was open for 0% of the time, Pallas kernels for 24%

profile of v2, /device:TPU:0, one launch (start us, length us, event | category | flops | bytes accessed | tf_op | source)
XLA Modules:
  0.0 33.5 jit_solution(10908133780346100602)
XLA Ops:
  0.6 1.0 %join.1 = (bf16[64,768]{1,0:T(8,128)(2,1)S(1)}, bf16[64,768]{1,0:T(8,128)(2,1)S(1)}, bf16[64,768]{1,0:T(8,128)(2,1)S(1)}, bf16[64,768]{1,0:T(8,128)(2,1)S(1)}, b...) custom-call(bf16[1,64,384]{2,1,0:T(8,128)(2,1)} %key_ref.1, bf16[1,64,384]{2,1,0:T(8,128)(2,1)} %value_ref.1, ...), custom_call_target="tpu_custom_call" | custom-call | tf_op jit(solution)/shard_map/join/pallas_call | solution.py:230
  1.7 3.1 %collective-permute-start = (bf16[64,768]{1,0:T(8,128)(2,1)S(1)}, bf16[64,768]{1,0:T(8,128)(2,1)S(1)}, u32[]{:S(2)}, u32[]{:S(2)}) collective-permute-start(bf16[64,768]{1,0:T(8,128)(2,1)S(1)} %get-tuple-element.25), channel_id=1, source_target_pairs={{0,2},{2,6},{4,0},{6,4},{1,3},{3,7},{5,1},{7,5},{8,10},{10,14},{12... | collective-permute-start | bytes 294920 | tf_op jit(solution)/shard_map/ppermute | solution.py:33
  4.8 1.1 %collective-permute-start.1 = (bf16[64,768]{1,0:T(8,128)(2,1)S(1)}, bf16[64,768]{1,0:T(8,128)(2,1)S(1)}, u32[]{:S(2)}, u32[]{:S(2)}) collective-permute-start(bf16[64,768]{1,0:T(8,128)(2,1)S(1)} %get-tuple-element.26), channel_id=1, source_target_pairs={{0,4},{2,0},{4,6},{6,2},{1,5},{3,1},{5,7},{7,3},{8,12},{10,8},{12,... | collective-permute-start | bytes 294920 | tf_op jit(solution)/shard_map/ppermute | solution.py:33
  5.8 0.7 %collective-permute-start.2 = (bf16[64,768]{1,0:T(8,128)(2,1)S(1)}, bf16[64,768]{1,0:T(8,128)(2,1)S(1)}, u32[]{:S(2)}, u32[]{:S(2)}) collective-permute-start(bf16[64,768]{1,0:T(8,128)(2,1)S(1)} %get-tuple-element.27), channel_id=1, source_target_pairs={{8,0},{16,8},{24,16},{0,24},{9,1},{17,9},{25,17},{1,25},{10,2},{18... | collective-permute-start | bytes 294920 | tf_op jit(solution)/shard_map/ppermute | solution.py:23
  6.5 1.2 %collective-permute-start.3 = (bf16[64,768]{1,0:T(8,128)(2,1)S(1)}, bf16[64,768]{1,0:T(8,128)(2,1)S(1)}, u32[]{:S(2)}, u32[]{:S(2)}) collective-permute-start(bf16[64,768]{1,0:T(8,128)(2,1)S(1)} %get-tuple-element.28), channel_id=1, source_target_pairs={{8,0},{16,8},{24,16},{0,24},{9,1},{17,9},{25,17},{1,25},{10,2},{18... | collective-permute-start | bytes 294920 | tf_op jit(solution)/shard_map/ppermute | solution.py:23
  7.7 3.6 %collective-permute-start.4 = (bf16[64,768]{1,0:T(8,128)(2,1)S(1)}, bf16[64,768]{1,0:T(8,128)(2,1)S(1)}, u32[]{:S(2)}, u32[]{:S(2)}) collective-permute-start(bf16[64,768]{1,0:T(8,128)(2,1)S(1)} %get-tuple-element.29), channel_id=1, source_target_pairs={{0,6},{2,4},{4,2},{6,0},{1,7},{3,5},{5,3},{7,1},{8,14},{10,12},{12... | collective-permute-start | bytes 294920 | tf_op jit(solution)/shard_map/ppermute | solution.py:33
  11.3 2.2 %stage.1 = (s32[8,128]{1,0:T(8,128)S(1)}, bf16[128,768]{1,0:T(8,128)(2,1)S(1)}, bf16[2688,768]{1,0:T(8,128)(2,1)S(1)}) custom-call(s32[4]{0:T(128)} %span_ref.1, s32[4]{0:T(128)} %prefix_ref.1, bf16[1,128,768]{2,1,0:T(8,128)(2,1)} %q_ref.1, bf16[1,5376,768]{2,1,0:T(8,128)(2,1)} %w_ref.3), custom_call_target="tpu_custom_call" | custom-call | tf_op jit(solution)/shard_map/stage/pallas_call | solution.py:245
  13.5 0.0 collective-permute-done.refs_1_
  13.5 0.0 collective-permute-done.1.refs_2_
  13.5 0.0 collective-permute-done.2.refs_3_.d_low
  13.6 0.0 collective-permute-done.3.refs_4_.d_high
  13.6 0.9 %collective-permute-done.4.refs_5_ = bf16[64,768]{1,0:T(8,128)(2,1)S(1)} collective-permute-done((bf16[64,768]{1,0:T(8,128)(2,1)S(1)}, bf16[64,768]{1,0:T(8,128)(2,1)S(1)}, u32[]{:S(2)}, u32[]{:S(2)}) %collective-permute-start.4) | collective-permute-done | bytes 98336 | tf_op jit(solution)/shard_map/ppermute | solution.py:33
  14.5 1.6 %attention.1 = (bf16[768,128]{1,0:T(8,128)(2,1)S(1)}, bf16[3,256,256]{2,1,0:T(8,128)(2,1)S(1)}, bf16[3,256,256]{2,1,0:T(8,128)(2,1)S(1)}, bf16[1504,128]{1,0:T(8,128)(2,1)S(1)}) custom-call(s32[8,128]{1,0:T(8,128)S(1)} %get-tuple-element.22.limit_ref, bf16[128,768]{1,0:T(8,128)(2,1)S(1)} %get-tuple-element.23.q_ref, ...), custom_call_target="tpu_custom_call" | custom-call | tf_op jit(solution)/shard_map/attention/pallas_call | solution.py:260
  16.1 1.6 %collective-permute-start.6 = (bf16[1504,128]{1,0:T(8,128)(2,1)S(1)}, bf16[1504,128]{1,0:T(8,128)(2,1)S(1)}, u32[]{:S(2)}, u32[]{:S(2)}) collective-permute-start(bf16[1504,128]{1,0:T(8,128)(2,1)S(1)} %get-tuple-element.32), channel_id=1, source_target_pairs={{1,0},{0,1},{3,2},{2,3},{5,4},{4,5},{7,6},{6,7},{9,8},{8,9},{11,10... | collective-permute-start | bytes 1155080 | tf_op jit(solution)/shard_map/ppermute | solution.py:23
  17.7 0.6 %rest.1 = bf16[1184,128]{1,0:T(8,128)(2,1)S(1)} custom-call(bf16[768,128]{1,0:T(8,128)(2,1)S(1)} %get-tuple-element.31.grad_ref, bf16[2688,768]{1,0:T(8,128)(2,1)S(1)} %get-tuple-element.30.refs_6_.refs_0_), custom_call_target="tpu_custom_call" | custom-call | tf_op jit(solution)/shard_map/rest/pallas_call | solution.py:266
  18.3 0.6 %collective-permute-start.5 = (bf16[1184,128]{1,0:T(8,128)(2,1)S(1)}, bf16[1184,128]{1,0:T(8,128)(2,1)S(1)}, u32[]{:S(2)}, u32[]{:S(2)}) collective-permute-start(bf16[1184,128]{1,0:T(8,128)(2,1)S(1)} %rest.1), channel_id=1, source_target_pairs={{1,0},{0,1},{3,2},{2,3},{5,4},{4,5},{7,6},{6,7},{9,8},{8,9},{11,10... | collective-permute-start | bytes 909320 | tf_op jit(solution)/shard_map/ppermute | solution.py:23
  18.9 0.4 %terms.1 = (bf16[64,768]{1,0:T(8,128)(2,1)S(1)}, bf16[64,768]{1,0:T(8,128)(2,1)S(1)}, bf16[64,768]{1,0:T(8,128)(2,1)S(1)}, bf16[64,768]{1,0:T(8,128)(2,1)S(1)}) custom-call(bf16[3,256,256]{2,1,0:T(8,128)(2,1)S(1)} %get-tuple-element.33.probs_ref, bf16[3,256,256]{2,1,0:T(8,128)(2,1)S(1)} %get-tuple-element.34.dscores_ref, ...), custom_call_target="tpu_custom_call" | custom-call | tf_op jit(solution)/shard_map/terms/pallas_call | solution.py:273
  19.2 3.2 %collective-permute-start.7 = (bf16[64,768]{1,0:T(8,128)(2,1)S(1)}, bf16[64,768]{1,0:T(8,128)(2,1)S(1)}, u32[]{:S(2)}, u32[]{:S(2)}) collective-permute-start(bf16[64,768]{1,0:T(8,128)(2,1)S(1)} %get-tuple-element.36), channel_id=1, source_target_pairs={{2,0},{6,2},{0,4},{4,6},{3,1},{7,3},{1,5},{5,7},{10,8},{14,10},{8,... | collective-permute-start | bytes 294920 | tf_op jit(solution)/shard_map/ppermute | solution.py:37
  22.4 0.0 collective-permute-start.8
  22.4 2.3 %collective-permute-start.9 = (bf16[64,768]{1,0:T(8,128)(2,1)S(1)}, bf16[64,768]{1,0:T(8,128)(2,1)S(1)}, u32[]{:S(2)}, u32[]{:S(2)}) collective-permute-start(bf16[64,768]{1,0:T(8,128)(2,1)S(1)} %get-tuple-element.38), channel_id=1, source_target_pairs={{6,0},{4,2},{2,4},{0,6},{7,1},{5,3},{3,5},{1,7},{14,8},{12,10},{10... | collective-permute-start | bytes 294920 | tf_op jit(solution)/shard_map/ppermute | solution.py:37
  24.7 3.4 %own.1.own_ref = f32[2688,128]{1,0:T(8,128)S(1)} custom-call(bf16[768,128]{1,0:T(8,128)(2,1)S(1)} %get-tuple-element.31.grad_ref, bf16[1,5376,768]{2,1,0:T(8,128)(2,1)} %w_ref.3), custom_call_target="tpu_custom_call" | custom-call | tf_op jit(solution)/shard_map/own/pallas_call | solution.py:281
  28.1 0.0 collective-permute-done.7.refs_1_
  28.1 2.8 %collective-permute-done.8.refs_2_ = bf16[64,768]{1,0:T(8,128)(2,1)S(1)} collective-permute-done((bf16[64,768]{1,0:T(8,128)(2,1)S(1)}, bf16[64,768]{1,0:T(8,128)(2,1)S(1)}, u32[]{:S(2)}, u32[]{:S(2)}) %collective-permute-start.8) | collective-permute-done | bytes 98336 | tf_op jit(solution)/shard_map/ppermute | solution.py:37
  30.9 0.0 collective-permute-done.9.refs_3_
  30.9 0.7 %term_sum.1 = (bf16[1,64,384]{2,1,0:T(8,128)(2,1)}, bf16[1,64,384]{2,1,0:T(8,128)(2,1)}) custom-call(bf16[64,768]{1,0:T(8,128)(2,1)S(1)} %get-tuple-element.35.refs_0_, bf16[64,768]{1,0:T(8,128)(2,1)S(1)} %collective-permute-done.7.refs_1_, bf16[64,768]{1,0:T(8,128)(2,1)S(1)} %collective-permute-done.8.refs_2_, ...), custom_call_target="tpu_custom_call" | custom-call | tf_op jit(solution)/shard_map/term_sum/pallas_call | solution.py:288
  31.6 0.0 collective-permute-done.6.refs_0_
  31.6 0.8 %input_sum.2.refs_1_ = bf16[1,2688,128]{2,1,0:T(8,128)(2,1)} custom-call(f32[2688,128]{1,0:T(8,128)S(1)} %own.1.own_ref, bf16[1504,128]{1,0:T(8,128)(2,1)S(1)} %collective-permute-done.6.refs_0_), custom_call_target="tpu_custom_call" | custom-call | tf_op jit(solution)/shard_map/input_sum/pallas_call | solution.py:294
  32.5 0.2 collective-permute-done.5.refs_0_
  32.7 0.8 %input_sum.3 = bf16[1,2688,128]{2,1,0:T(8,128)(2,1)} custom-call(f32[2688,128]{1,0:T(8,128)S(1)} %own.1.own_ref, bf16[1184,128]{1,0:T(8,128)(2,1)S(1)} %collective-permute-done.5.refs_0_, bf16[1,2688,128]{2,1,0:T(8,128)(2,1)} %input_sum.2.refs_1_), custom_call_target="tpu_custom_call", output_to_operand_aliasing={{}: (2, {})} | custom-call | tf_op jit(solution)/shard_map/input_sum/pallas_call | solution.py:294
Async XLA Ops:
  1.7 11.9 %collective-permute-start = (bf16[64,768]{1,0:T(8,128)(2,1)S(1)}, bf16[64,768]{1,0:T(8,128)(2,1)S(1)}, u32[]{:S(2)}, u32[]{:S(2)}) collective-permute-start(bf16[64,768]{1,0:T(8,128)(2,1)S(1)} %get-tuple-element.25), channel_id=1, source_target_pairs={{0,2},{2,6},{4,0},{6,4},{1,3},{3,7},{5,1},{7,5},{8,10},{10,14},{12... | collective-permute-start | bytes 294920 | tf_op jit(solution)/shard_map/ppermute | solution.py:33
  4.8 8.8 %collective-permute-start.1 = (bf16[64,768]{1,0:T(8,128)(2,1)S(1)}, bf16[64,768]{1,0:T(8,128)(2,1)S(1)}, u32[]{:S(2)}, u32[]{:S(2)}) collective-permute-start(bf16[64,768]{1,0:T(8,128)(2,1)S(1)} %get-tuple-element.26), channel_id=1, source_target_pairs={{0,4},{2,0},{4,6},{6,2},{1,5},{3,1},{5,7},{7,3},{8,12},{10,8},{12,... | collective-permute-start | bytes 294920 | tf_op jit(solution)/shard_map/ppermute | solution.py:33
  5.8 7.7 %collective-permute-start.2 = (bf16[64,768]{1,0:T(8,128)(2,1)S(1)}, bf16[64,768]{1,0:T(8,128)(2,1)S(1)}, u32[]{:S(2)}, u32[]{:S(2)}) collective-permute-start(bf16[64,768]{1,0:T(8,128)(2,1)S(1)} %get-tuple-element.27), channel_id=1, source_target_pairs={{8,0},{16,8},{24,16},{0,24},{9,1},{17,9},{25,17},{1,25},{10,2},{18... | collective-permute-start | bytes 294920 | tf_op jit(solution)/shard_map/ppermute | solution.py:23
  6.5 7.1 %collective-permute-start.3 = (bf16[64,768]{1,0:T(8,128)(2,1)S(1)}, bf16[64,768]{1,0:T(8,128)(2,1)S(1)}, u32[]{:S(2)}, u32[]{:S(2)}) collective-permute-start(bf16[64,768]{1,0:T(8,128)(2,1)S(1)} %get-tuple-element.28), channel_id=1, source_target_pairs={{8,0},{16,8},{24,16},{0,24},{9,1},{17,9},{25,17},{1,25},{10,2},{18... | collective-permute-start | bytes 294920 | tf_op jit(solution)/shard_map/ppermute | solution.py:23
  7.7 6.7 %collective-permute-start.4 = (bf16[64,768]{1,0:T(8,128)(2,1)S(1)}, bf16[64,768]{1,0:T(8,128)(2,1)S(1)}, u32[]{:S(2)}, u32[]{:S(2)}) collective-permute-start(bf16[64,768]{1,0:T(8,128)(2,1)S(1)} %get-tuple-element.29), channel_id=1, source_target_pairs={{0,6},{2,4},{4,2},{6,0},{1,7},{3,5},{5,3},{7,1},{8,14},{10,12},{12... | collective-permute-start | bytes 294920 | tf_op jit(solution)/shard_map/ppermute | solution.py:33
  16.1 15.5 %collective-permute-start.6 = (bf16[1504,128]{1,0:T(8,128)(2,1)S(1)}, bf16[1504,128]{1,0:T(8,128)(2,1)S(1)}, u32[]{:S(2)}, u32[]{:S(2)}) collective-permute-start(bf16[1504,128]{1,0:T(8,128)(2,1)S(1)} %get-tuple-element.32), channel_id=1, source_target_pairs={{1,0},{0,1},{3,2},{2,3},{5,4},{4,5},{7,6},{6,7},{9,8},{8,9},{11,10... | collective-permute-start | bytes 1155080 | tf_op jit(solution)/shard_map/ppermute | solution.py:23
  18.3 14.4 %collective-permute-start.5 = (bf16[1184,128]{1,0:T(8,128)(2,1)S(1)}, bf16[1184,128]{1,0:T(8,128)(2,1)S(1)}, u32[]{:S(2)}, u32[]{:S(2)}) collective-permute-start(bf16[1184,128]{1,0:T(8,128)(2,1)S(1)} %rest.1), channel_id=1, source_target_pairs={{1,0},{0,1},{3,2},{2,3},{5,4},{4,5},{7,6},{6,7},{9,8},{8,9},{11,10... | collective-permute-start | bytes 909320 | tf_op jit(solution)/shard_map/ppermute | solution.py:23
  19.2 8.9 %collective-permute-start.7 = (bf16[64,768]{1,0:T(8,128)(2,1)S(1)}, bf16[64,768]{1,0:T(8,128)(2,1)S(1)}, u32[]{:S(2)}, u32[]{:S(2)}) collective-permute-start(bf16[64,768]{1,0:T(8,128)(2,1)S(1)} %get-tuple-element.36), channel_id=1, source_target_pairs={{2,0},{6,2},{0,4},{4,6},{3,1},{7,3},{1,5},{5,7},{10,8},{14,10},{8,... | collective-permute-start | bytes 294920 | tf_op jit(solution)/shard_map/ppermute | solution.py:37
  22.4 8.5 %collective-permute-start.8 = (bf16[64,768]{1,0:T(8,128)(2,1)S(1)}, bf16[64,768]{1,0:T(8,128)(2,1)S(1)}, u32[]{:S(2)}, u32[]{:S(2)}) collective-permute-start(bf16[64,768]{1,0:T(8,128)(2,1)S(1)} %get-tuple-element.37), channel_id=1, source_target_pairs={{4,0},{0,2},{6,4},{2,6},{5,1},{1,3},{7,5},{3,7},{12,8},{8,10},{14,... | collective-permute-start | bytes 294920 | tf_op jit(solution)/shard_map/ppermute | solution.py:37
  22.4 8.5 %collective-permute-start.9 = (bf16[64,768]{1,0:T(8,128)(2,1)S(1)}, bf16[64,768]{1,0:T(8,128)(2,1)S(1)}, u32[]{:S(2)}, u32[]{:S(2)}) collective-permute-start(bf16[64,768]{1,0:T(8,128)(2,1)S(1)} %get-tuple-element.38), channel_id=1, source_target_pairs={{6,0},{4,2},{2,4},{0,6},{7,1},{5,3},{3,5},{1,7},{14,8},{12,10},{10... | collective-permute-start | bytes 294920 | tf_op jit(solution)/shard_map/ppermute | solution.py:37

commit v3 on v1

--- a/solution.py
+++ b/solution.py
@@ -101,10 +101,9 @@
 
 
 def attention_kernel(partners, n_other, limit_ref, q_ref, *refs):
-    most = 1 + len(partners[:-1])
+    most = 1 + len(partners[:1])
     kv_refs, (d_low, d_high), refs = refs[:most], refs[most : most + 2], refs[most + 2 :]
-    if partners:
-        kv_refs, refs = kv_refs + refs[:1], refs[1:]
+    kv_refs, refs = kv_refs + refs[: len(partners[1:])], refs[len(partners[1:]) :]
     w_refs = refs[:n_other]
     grad_ref, probs_ref, dscores_ref, *part_refs = refs[n_other:]
 
@@ -224,7 +223,7 @@
     def shape(*dims, dtype=low):
         return jax.ShapeDtypeStruct(dims, dtype)
 
-    first = feats // 16 * 9 // 16 * 16
+    first = feats // 16 * 17 // 32 * 16
     partners = seq_steps(n_seq) if direct else []
     n_copies = 1 + len(partners)
     *joined, grad_low, grad_high = kernel_call(
@@ -235,11 +234,11 @@
         [pltpu.SemaphoreType.DMA((4,))],
     )(*[in_hbm(x) for x in (keys, values, grad_out)])
     if direct:
-        blocks = joined[-1:] + [sent(x, step) for x, step in zip(joined, partners[:-1])]
+        blocks = joined[-1:] + [sent(x, step) for x, step in zip(joined, partners[:1])]
     else:
         blocks = [lax.all_gather(joined[0], "seq", axis=0, tiled=True)]
     incoming = [shifted(part, "section", -1) for part in (grad_low, grad_high)]
-    last = [sent(joined[len(partners) - 1], step) for step in partners[-1:]]
+    last = [sent(x, step) for x, step in zip(joined[1:], partners[1:])]
     n_blocks, block_rows = len(blocks) + len(last), blocks[0].shape[0]
 
     limit, q, *w_other = kernel_call(

time: 33.3 us -> 34.5 us (1.036)
  waiting for transfers between devices: 5.14 us -> 6.05 us
    ppermute x3, waiting for transfers between devices: 1.22 us -> 1.88 us  [sent(): return lax.ppermute(block, 'seq', list(enumerate(step)))]
  transfers between devices with their start and end apart: 10 -> 10, of which waited for: 3 -> 4; matrix products, arithmetic and copies ran while one was open for 0% -> 0% of each run, Pallas kernels for 25% -> 24%
where the time goes in v3:
time: 34.5 us; the launch traced here: 34.3 us
  starting transfers between devices  16 us (46%)
  Pallas kernels  11.6 us (34%)
  waiting for transfers between devices  6.05 us (18%)
  between operations  0.73 us (2%)
    ppermute x3, starting transfers between devices, sent(): return lax.ppermute(block, 'seq', list(enumerate(step)))  7.13 us
    ppermute x3, starting transfers between devices, sent_back(): return lax.ppermute(block, 'seq', [(to, i) for i, to in enumerate(step)])  5.08 us
    ppermute x3, waiting for transfers between devices, sent_back(): return lax.ppermute(block, 'seq', [(to, i) for i, to in enumerate(step)])  4.17 us
    ppermute x4, starting transfers between devices, shifted(): return lax.ppermute(block, axis, route)  3.76 us
    pallas_call x1, Pallas kernels, on_device(): kernel_call(functools.partial(own_kernel, n_head), 'own', shape(feats, ro...  3.41 us
    pallas_call x1, Pallas kernels, on_device(): kernel_call(functools.partial(stage_kernel, n_head), 'stage', [shape(8, H...  2.21 us
    ppermute x3, waiting for transfers between devices, sent(): return lax.ppermute(block, 'seq', list(enumerate(step)))  1.88 us
    pallas_call x2, Pallas kernels, on_device(): pl.pallas_call(functools.partial(input_sum_kernel, n_other, start), out_s...  1.6 us
  transfers between devices with their start and end apart: 10, of which 4 were waited for; matrix products, arithmetic and copies ran while one was open for 0% of the time, Pallas kernels for 24%

profile of v3, /device:TPU:0, one launch (start us, length us, event | category | flops | bytes accessed | tf_op | source)
XLA Modules:
  0.0 34.3 jit_solution(13291123814376690632)
XLA Ops:
  0.6 1.0 %join.1 = (bf16[64,768]{1,0:T(8,128)(2,1)S(1)}, bf16[64,768]{1,0:T(8,128)(2,1)S(1)}, bf16[64,768]{1,0:T(8,128)(2,1)S(1)}, bf16[64,768]{1,0:T(8,128)(2,1)S(1)}, b...) custom-call(bf16[1,64,384]{2,1,0:T(8,128)(2,1)} %key_ref.1, bf16[1,64,384]{2,1,0:T(8,128)(2,1)} %value_ref.1, ...), custom_call_target="tpu_custom_call" | custom-call | tf_op jit(solution)/shard_map/join/pallas_call | solution.py:229
  1.7 3.1 %collective-permute-start = (bf16[64,768]{1,0:T(8,128)(2,1)S(1)}, bf16[64,768]{1,0:T(8,128)(2,1)S(1)}, u32[]{:S(2)}, u32[]{:S(2)}) collective-permute-start(bf16[64,768]{1,0:T(8,128)(2,1)S(1)} %get-tuple-element.25), channel_id=1, source_target_pairs={{0,2},{2,6},{4,0},{6,4},{1,3},{3,7},{5,1},{7,5},{8,10},{10,14},{12... | collective-permute-start | bytes 294920 | tf_op jit(solution)/shard_map/ppermute | solution.py:33
  4.8 0.7 %collective-permute-start.1 = (bf16[64,768]{1,0:T(8,128)(2,1)S(1)}, bf16[64,768]{1,0:T(8,128)(2,1)S(1)}, u32[]{:S(2)}, u32[]{:S(2)}) collective-permute-start(bf16[64,768]{1,0:T(8,128)(2,1)S(1)} %get-tuple-element.26), channel_id=1, source_target_pairs={{8,0},{16,8},{24,16},{0,24},{9,1},{17,9},{25,17},{1,25},{10,2},{18... | collective-permute-start | bytes 294920 | tf_op jit(solution)/shard_map/ppermute | solution.py:23
  5.4 1.0 %collective-permute-start.2 = (bf16[64,768]{1,0:T(8,128)(2,1)S(1)}, bf16[64,768]{1,0:T(8,128)(2,1)S(1)}, u32[]{:S(2)}, u32[]{:S(2)}) collective-permute-start(bf16[64,768]{1,0:T(8,128)(2,1)S(1)} %get-tuple-element.27), channel_id=1, source_target_pairs={{8,0},{16,8},{24,16},{0,24},{9,1},{17,9},{25,17},{1,25},{10,2},{18... | collective-permute-start | bytes 294920 | tf_op jit(solution)/shard_map/ppermute | solution.py:23
  6.4 2.5 %collective-permute-start.3 = (bf16[64,768]{1,0:T(8,128)(2,1)S(1)}, bf16[64,768]{1,0:T(8,128)(2,1)S(1)}, u32[]{:S(2)}, u32[]{:S(2)}) collective-permute-start(bf16[64,768]{1,0:T(8,128)(2,1)S(1)} %get-tuple-element.28), channel_id=1, source_target_pairs={{0,6},{2,4},{4,2},{6,0},{1,7},{3,5},{5,3},{7,1},{8,14},{10,12},{12... | collective-permute-start | bytes 294920 | tf_op jit(solution)/shard_map/ppermute | solution.py:33
  8.8 1.6 %collective-permute-start.4 = (bf16[64,768]{1,0:T(8,128)(2,1)S(1)}, bf16[64,768]{1,0:T(8,128)(2,1)S(1)}, u32[]{:S(2)}, u32[]{:S(2)}) collective-permute-start(bf16[64,768]{1,0:T(8,128)(2,1)S(1)} %get-tuple-element.29), channel_id=1, source_target_pairs={{0,4},{2,0},{4,6},{6,2},{1,5},{3,1},{5,7},{7,3},{8,12},{10,8},{12,... | collective-permute-start | bytes 294920 | tf_op jit(solution)/shard_map/ppermute | solution.py:33
  10.4 2.2 %stage.1 = (s32[8,128]{1,0:T(8,128)S(1)}, bf16[128,768]{1,0:T(8,128)(2,1)S(1)}, bf16[2688,768]{1,0:T(8,128)(2,1)S(1)}) custom-call(s32[4]{0:T(128)} %span_ref.1, s32[4]{0:T(128)} %prefix_ref.1, bf16[1,128,768]{2,1,0:T(8,128)(2,1)} %q_ref.1, bf16[1,5376,768]{2,1,0:T(8,128)(2,1)} %w_ref.3), custom_call_target="tpu_custom_call" | custom-call | tf_op jit(solution)/shard_map/stage/pallas_call | solution.py:244
  12.6 0.0 collective-permute-done.refs_1_
  12.6 0.0 collective-permute-done.1.refs_2_.d_low
  12.6 0.0 collective-permute-done.2.refs_3_.d_high
  12.7 1.0 %collective-permute-done.3.refs_4_ = bf16[64,768]{1,0:T(8,128)(2,1)S(1)} collective-permute-done((bf16[64,768]{1,0:T(8,128)(2,1)S(1)}, bf16[64,768]{1,0:T(8,128)(2,1)S(1)}, u32[]{:S(2)}, u32[]{:S(2)}) %collective-permute-start.3) | collective-permute-done | bytes 98336 | tf_op jit(solution)/shard_map/ppermute | solution.py:33
  13.6 0.9 %collective-permute-done.4.refs_5_ = bf16[64,768]{1,0:T(8,128)(2,1)S(1)} collective-permute-done((bf16[64,768]{1,0:T(8,128)(2,1)S(1)}, bf16[64,768]{1,0:T(8,128)(2,1)S(1)}, u32[]{:S(2)}, u32[]{:S(2)}) %collective-permute-start.4) | collective-permute-done | bytes 98336 | tf_op jit(solution)/shard_map/ppermute | solution.py:33
  14.5 1.6 %attention.1 = (bf16[768,128]{1,0:T(8,128)(2,1)S(1)}, bf16[3,256,256]{2,1,0:T(8,128)(2,1)S(1)}, bf16[3,256,256]{2,1,0:T(8,128)(2,1)S(1)}, bf16[1424,128]{1,0:T(8,128)(2,1)S(1)}) custom-call(s32[8,128]{1,0:T(8,128)S(1)} %get-tuple-element.22.limit_ref, bf16[128,768]{1,0:T(8,128)(2,1)S(1)} %get-tuple-element.23.q_ref, ...), custom_call_target="tpu_custom_call" | custom-call | tf_op jit(solution)/shard_map/attention/pallas_call | solution.py:259
  16.1 1.6 %collective-permute-start.6 = (bf16[1424,128]{1,0:T(8,128)(2,1)S(1)}, bf16[1424,128]{1,0:T(8,128)(2,1)S(1)}, u32[]{:S(2)}, u32[]{:S(2)}) collective-permute-start(bf16[1424,128]{1,0:T(8,128)(2,1)S(1)} %get-tuple-element.32), channel_id=1, source_target_pairs={{1,0},{0,1},{3,2},{2,3},{5,4},{4,5},{7,6},{6,7},{9,8},{8,9},{11,10... | collective-permute-start | bytes 1093640 | tf_op jit(solution)/shard_map/ppermute | solution.py:23
  17.7 0.7 %rest.1 = bf16[1264,128]{1,0:T(8,128)(2,1)S(1)} custom-call(bf16[768,128]{1,0:T(8,128)(2,1)S(1)} %get-tuple-element.31.grad_ref, bf16[2688,768]{1,0:T(8,128)(2,1)S(1)} %get-tuple-element.30.refs_6_.refs_0_), custom_call_target="tpu_custom_call" | custom-call | tf_op jit(solution)/shard_map/rest/pallas_call | solution.py:265
  18.4 0.6 %collective-permute-start.5 = (bf16[1264,128]{1,0:T(8,128)(2,1)S(1)}, bf16[1264,128]{1,0:T(8,128)(2,1)S(1)}, u32[]{:S(2)}, u32[]{:S(2)}) collective-permute-start(bf16[1264,128]{1,0:T(8,128)(2,1)S(1)} %rest.1), channel_id=1, source_target_pairs={{1,0},{0,1},{3,2},{2,3},{5,4},{4,5},{7,6},{6,7},{9,8},{8,9},{11,10... | collective-permute-start | bytes 970760 | tf_op jit(solution)/shard_map/ppermute | solution.py:23
  19.0 0.4 %terms.1 = (bf16[64,768]{1,0:T(8,128)(2,1)S(1)}, bf16[64,768]{1,0:T(8,128)(2,1)S(1)}, bf16[64,768]{1,0:T(8,128)(2,1)S(1)}, bf16[64,768]{1,0:T(8,128)(2,1)S(1)}) custom-call(bf16[3,256,256]{2,1,0:T(8,128)(2,1)S(1)} %get-tuple-element.33.probs_ref, bf16[3,256,256]{2,1,0:T(8,128)(2,1)S(1)} %get-tuple-element.34.dscores_ref, ...), custom_call_target="tpu_custom_call" | custom-call | tf_op jit(solution)/shard_map/terms/pallas_call | solution.py:272
  19.3 3.2 %collective-permute-start.7 = (bf16[64,768]{1,0:T(8,128)(2,1)S(1)}, bf16[64,768]{1,0:T(8,128)(2,1)S(1)}, u32[]{:S(2)}, u32[]{:S(2)}) collective-permute-start(bf16[64,768]{1,0:T(8,128)(2,1)S(1)} %get-tuple-element.36), channel_id=1, source_target_pairs={{2,0},{6,2},{0,4},{4,6},{3,1},{7,3},{1,5},{5,7},{10,8},{14,10},{8,... | collective-permute-start | bytes 294920 | tf_op jit(solution)/shard_map/ppermute | solution.py:37
  22.6 1.8 %collective-permute-start.8 = (bf16[64,768]{1,0:T(8,128)(2,1)S(1)}, bf16[64,768]{1,0:T(8,128)(2,1)S(1)}, u32[]{:S(2)}, u32[]{:S(2)}) collective-permute-start(bf16[64,768]{1,0:T(8,128)(2,1)S(1)} %get-tuple-element.37), channel_id=1, source_target_pairs={{6,0},{4,2},{2,4},{0,6},{7,1},{5,3},{3,5},{1,7},{14,8},{12,10},{10... | collective-permute-start | bytes 294920 | tf_op jit(solution)/shard_map/ppermute | solution.py:37
  24.4 0.0 collective-permute-start.9
  24.4 3.4 %own.1.own_ref = f32[2688,128]{1,0:T(8,128)S(1)} custom-call(bf16[768,128]{1,0:T(8,128)(2,1)S(1)} %get-tuple-element.31.grad_ref, bf16[1,5376,768]{2,1,0:T(8,128)(2,1)} %w_ref.3), custom_call_target="tpu_custom_call" | custom-call | tf_op jit(solution)/shard_map/own/pallas_call | solution.py:280
  27.8 0.0 collective-permute-done.7.refs_1_
  27.8 2.0 %collective-permute-done.8.refs_2_ = bf16[64,768]{1,0:T(8,128)(2,1)S(1)} collective-permute-done((bf16[64,768]{1,0:T(8,128)(2,1)S(1)}, bf16[64,768]{1,0:T(8,128)(2,1)S(1)}, u32[]{:S(2)}, u32[]{:S(2)}) %collective-permute-start.8) | collective-permute-done | bytes 98336 | tf_op jit(solution)/shard_map/ppermute | solution.py:37
  29.8 2.2 %collective-permute-done.9.refs_3_ = bf16[64,768]{1,0:T(8,128)(2,1)S(1)} collective-permute-done((bf16[64,768]{1,0:T(8,128)(2,1)S(1)}, bf16[64,768]{1,0:T(8,128)(2,1)S(1)}, u32[]{:S(2)}, u32[]{:S(2)}) %collective-permute-start.9) | collective-permute-done | bytes 98336 | tf_op jit(solution)/shard_map/ppermute | solution.py:37
  32.0 0.7 %term_sum.1 = (bf16[1,64,384]{2,1,0:T(8,128)(2,1)}, bf16[1,64,384]{2,1,0:T(8,128)(2,1)}) custom-call(bf16[64,768]{1,0:T(8,128)(2,1)S(1)} %get-tuple-element.35.refs_0_, bf16[64,768]{1,0:T(8,128)(2,1)S(1)} %collective-permute-done.7.refs_1_, bf16[64,768]{1,0:T(8,128)(2,1)S(1)} %collective-permute-done.8.refs_2_, ...), custom_call_target="tpu_custom_call" | custom-call | tf_op jit(solution)/shard_map/term_sum/pallas_call | solution.py:287
  32.7 0.0 collective-permute-done.6.refs_0_
  32.7 0.8 %input_sum.2.refs_1_ = bf16[1,2688,128]{2,1,0:T(8,128)(2,1)} custom-call(f32[2688,128]{1,0:T(8,128)S(1)} %own.1.own_ref, bf16[1424,128]{1,0:T(8,128)(2,1)S(1)} %collective-permute-done.6.refs_0_), custom_call_target="tpu_custom_call" | custom-call | tf_op jit(solution)/shard_map/input_sum/pallas_call | solution.py:293
  33.5 0.0 collective-permute-done.5.refs_0_
  33.5 0.8 %input_sum.3 = bf16[1,2688,128]{2,1,0:T(8,128)(2,1)} custom-call(f32[2688,128]{1,0:T(8,128)S(1)} %own.1.own_ref, bf16[1264,128]{1,0:T(8,128)(2,1)S(1)} %collective-permute-done.5.refs_0_, bf16[1,2688,128]{2,1,0:T(8,128)(2,1)} %input_sum.2.refs_1_), custom_call_target="tpu_custom_call", output_to_operand_aliasing={{}: (2, {})} | custom-call | tf_op jit(solution)/shard_map/input_sum/pallas_call | solution.py:293
Async XLA Ops:
  1.7 11.0 %collective-permute-start = (bf16[64,768]{1,0:T(8,128)(2,1)S(1)}, bf16[64,768]{1,0:T(8,128)(2,1)S(1)}, u32[]{:S(2)}, u32[]{:S(2)}) collective-permute-start(bf16[64,768]{1,0:T(8,128)(2,1)S(1)} %get-tuple-element.25), channel_id=1, source_target_pairs={{0,2},{2,6},{4,0},{6,4},{1,3},{3,7},{5,1},{7,5},{8,10},{10,14},{12... | collective-permute-start | bytes 294920 | tf_op jit(solution)/shard_map/ppermute | solution.py:33
  4.8 7.9 %collective-permute-start.1 = (bf16[64,768]{1,0:T(8,128)(2,1)S(1)}, bf16[64,768]{1,0:T(8,128)(2,1)S(1)}, u32[]{:S(2)}, u32[]{:S(2)}) collective-permute-start(bf16[64,768]{1,0:T(8,128)(2,1)S(1)} %get-tuple-element.26), channel_id=1, source_target_pairs={{8,0},{16,8},{24,16},{0,24},{9,1},{17,9},{25,17},{1,25},{10,2},{18... | collective-permute-start | bytes 294920 | tf_op jit(solution)/shard_map/ppermute | solution.py:23
  5.4 7.2 %collective-permute-start.2 = (bf16[64,768]{1,0:T(8,128)(2,1)S(1)}, bf16[64,768]{1,0:T(8,128)(2,1)S(1)}, u32[]{:S(2)}, u32[]{:S(2)}) collective-permute-start(bf16[64,768]{1,0:T(8,128)(2,1)S(1)} %get-tuple-element.27), channel_id=1, source_target_pairs={{8,0},{16,8},{24,16},{0,24},{9,1},{17,9},{25,17},{1,25},{10,2},{18... | collective-permute-start | bytes 294920 | tf_op jit(solution)/shard_map/ppermute | solution.py:23
  6.4 7.3 %collective-permute-start.3 = (bf16[64,768]{1,0:T(8,128)(2,1)S(1)}, bf16[64,768]{1,0:T(8,128)(2,1)S(1)}, u32[]{:S(2)}, u32[]{:S(2)}) collective-permute-start(bf16[64,768]{1,0:T(8,128)(2,1)S(1)} %get-tuple-element.28), channel_id=1, source_target_pairs={{0,6},{2,4},{4,2},{6,0},{1,7},{3,5},{5,3},{7,1},{8,14},{10,12},{12... | collective-permute-start | bytes 294920 | tf_op jit(solution)/shard_map/ppermute | solution.py:33
  8.8 5.7 %collective-permute-start.4 = (bf16[64,768]{1,0:T(8,128)(2,1)S(1)}, bf16[64,768]{1,0:T(8,128)(2,1)S(1)}, u32[]{:S(2)}, u32[]{:S(2)}) collective-permute-start(bf16[64,768]{1,0:T(8,128)(2,1)S(1)} %get-tuple-element.29), channel_id=1, source_target_pairs={{0,4},{2,0},{4,6},{6,2},{1,5},{3,1},{5,7},{7,3},{8,12},{10,8},{12,... | collective-permute-start | bytes 294920 | tf_op jit(solution)/shard_map/ppermute | solution.py:33
  16.1 16.6 %collective-permute-start.6 = (bf16[1424,128]{1,0:T(8,128)(2,1)S(1)}, bf16[1424,128]{1,0:T(8,128)(2,1)S(1)}, u32[]{:S(2)}, u32[]{:S(2)}) collective-permute-start(bf16[1424,128]{1,0:T(8,128)(2,1)S(1)} %get-tuple-element.32), channel_id=1, source_target_pairs={{1,0},{0,1},{3,2},{2,3},{5,4},{4,5},{7,6},{6,7},{9,8},{8,9},{11,10... | collective-permute-start | bytes 1093640 | tf_op jit(solution)/shard_map/ppermute | solution.py:23
  18.4 15.1 %collective-permute-start.5 = (bf16[1264,128]{1,0:T(8,128)(2,1)S(1)}, bf16[1264,128]{1,0:T(8,128)(2,1)S(1)}, u32[]{:S(2)}, u32[]{:S(2)}) collective-permute-start(bf16[1264,128]{1,0:T(8,128)(2,1)S(1)} %rest.1), channel_id=1, source_target_pairs={{1,0},{0,1},{3,2},{2,3},{5,4},{4,5},{7,6},{6,7},{9,8},{8,9},{11,10... | collective-permute-start | bytes 970760 | tf_op jit(solution)/shard_map/ppermute | solution.py:23
  19.3 8.5 %collective-permute-start.7 = (bf16[64,768]{1,0:T(8,128)(2,1)S(1)}, bf16[64,768]{1,0:T(8,128)(2,1)S(1)}, u32[]{:S(2)}, u32[]{:S(2)}) collective-permute-start(bf16[64,768]{1,0:T(8,128)(2,1)S(1)} %get-tuple-element.36), channel_id=1, source_target_pairs={{2,0},{6,2},{0,4},{4,6},{3,1},{7,3},{1,5},{5,7},{10,8},{14,10},{8,... | collective-permute-start | bytes 294920 | tf_op jit(solution)/shard_map/ppermute | solution.py:37
  22.6 7.2 %collective-permute-start.8 = (bf16[64,768]{1,0:T(8,128)(2,1)S(1)}, bf16[64,768]{1,0:T(8,128)(2,1)S(1)}, u32[]{:S(2)}, u32[]{:S(2)}) collective-permute-start(bf16[64,768]{1,0:T(8,128)(2,1)S(1)} %get-tuple-element.37), channel_id=1, source_target_pairs={{6,0},{4,2},{2,4},{0,6},{7,1},{5,3},{3,5},{1,7},{14,8},{12,10},{10... | collective-permute-start | bytes 294920 | tf_op jit(solution)/shard_map/ppermute | solution.py:37
  24.4 7.6 %collective-permute-start.9 = (bf16[64,768]{1,0:T(8,128)(2,1)S(1)}, bf16[64,768]{1,0:T(8,128)(2,1)S(1)}, u32[]{:S(2)}, u32[]{:S(2)}) collective-permute-start(bf16[64,768]{1,0:T(8,128)(2,1)S(1)} %get-tuple-element.38), channel_id=1, source_target_pairs={{4,0},{0,2},{6,4},{2,6},{5,1},{1,3},{7,5},{3,7},{12,8},{8,10},{14,... | collective-permute-start | bytes 294920 | tf_op jit(solution)/shard_map/ppermute | solution.py:37
